TPU v7x, 512 devices: a whole 4x8x8 slice. The times are simulated.
512 devices in a mesh: ta: 4 (over x), ha: 4 (over y_hi), wa: 32 (over z, y_lo, core).
Axes of the slice: x: 4, y: 8 (y_hi: 4, y_lo: 2; y = y_hi * 2 + y_lo), z: 8, core: 2. Of those that a mesh axis runs over, the one named last changes fastest.
Arguments:
- teacher_in: bfloat16 [8, 128, 256, 192], P('ta', 'ha', 'wa'), may hold values from -3 to 3
- teacher_weights: bfloat16 [1, 2, 3, 3, 3, 192, 192], replicated, may hold values from -0.4375 to 0.4375
- student_in: bfloat16 [8, 128, 256, 128], P('ta', ('ha', 'wa')), may hold values from -6 to 6
- depth_weights: float32 [4, 3, 3, 3, 128], replicated, may hold values from -1.25 to 1.25
- point_weights: bfloat16 [4, 128, 128], replicated, may hold values from -0.5 to 0.5
- project_weight: bfloat16 [128, 192], replicated, may hold values from -0.5 to 0.5
Outputs:
- voxel_grad: bfloat16 [8, 128, 256, 128], P('ta', ('ha', 'wa'))
All inputs are finite; a program needn't handle non-finite values.
Results may differ from a plain program's by a relative error of at most 0.01.
Values may be sent and summed in bfloat16 or wider, within the bound.
A program may use at most 128 MiB of HBM per device.

v0:
```python
import jax
import jax.numpy as jnp
from jax import lax
from jax.sharding import PartitionSpec as P


def from_behind(block, axis, distance):
    devices = range(lax.axis_size(axis))
    route = [(i - distance, i) for i in devices if i - distance in devices]
    return lax.ppermute(block, axis, route)


def extended_2(block, sides, width):
    for axis, dim in sides:
        count = lax.axis_size(axis)
        forward = [(i, i + 1) for i in range(count - 1)]
        backward = [(target, source) for source, target in forward]
        low = lax.ppermute(
            lax.slice_in_dim(block, block.shape[dim] - width, None, axis=dim), axis, forward
        )
        high = lax.ppermute(lax.slice_in_dim(block, 0, width, axis=dim), axis, backward)
        block = jnp.concatenate([low, block, high], axis=dim)
    return block


def root_norm(field):
    return field * lax.rsqrt(jnp.mean(field * field, axis=-1, keepdims=True) + 1e-06)


def silu_slope(field):
    sigmoid_value = jax.nn.sigmoid(field)
    return sigmoid_value * (1.0 + field * (1.0 - sigmoid_value))


def dense_conv(extended, kernel):
    frame_count = extended.shape[0] - 2
    row_count = extended.shape[1] - 2
    col_count = extended.shape[2] - 2
    channels = kernel.shape[-1]
    tap_list = []
    for step_t in range(3):
        for step_h in range(3):
            for step_w in range(3):
                tap_list.append(
                    extended[
                        step_t : step_t + frame_count,
                        step_h : step_h + row_count,
                        step_w : step_w + col_count,
                    ]
                )
    stacked = jnp.concatenate(tap_list, axis=-1).reshape(frame_count * row_count * col_count, -1)
    summed = jnp.dot(stacked, kernel.reshape(-1, channels), preferred_element_type=jnp.float32)
    return summed.reshape(frame_count, row_count, col_count, channels)


def depthwise(extended, kernel):
    frame_count = extended.shape[0] - 2
    row_count = extended.shape[1] - 2
    col_count = extended.shape[2] - 2
    summed = jnp.zeros((frame_count, row_count, col_count, kernel.shape[-1]), jnp.float32)
    for step_t in range(3):
        for step_h in range(3):
            for step_w in range(3):
                tap_slice = extended[
                    step_t : step_t + frame_count,
                    step_h : step_h + row_count,
                    step_w : step_w + col_count,
                ]
                summed = summed + tap_slice.astype(jnp.float32) * kernel[step_t, step_h, step_w]
    return summed


def teacher_extend(active):
    earlier = from_behind(active, "ta", 1)
    longer = jnp.concatenate([earlier, active], axis=0)
    return extended_2(longer, (("ha", 1), ("wa", 2)), 1)


def rows_border(longer):
    widened = extended_2(longer, ((("ha", "wa"), 1),), 1)
    return jnp.pad(widened, ((0, 0), (0, 0), (1, 1), (0, 0)))


def rows_extend_past(active):
    earlier = from_behind(active, "ta", 1)
    return rows_border(jnp.concatenate([earlier, active], axis=0))


def rows_extend_future(backward):
    upcoming = from_behind(backward, "ta", -1)
    return rows_border(jnp.concatenate([backward, upcoming], axis=0))


def student_pass(
    initial, target, depth_weights, point_weights, project_weight, extend_past, extend_future
):
    channels = initial.shape[-1]
    current = initial.astype(jnp.float32)
    stored = []
    for layer_index in range(depth_weights.shape[0]):
        active = jax.nn.silu(current).astype(jnp.bfloat16)
        spread = depthwise(extend_past(active), depth_weights[layer_index]).astype(jnp.bfloat16)
        stored.append(current)
        mixed = jnp.dot(
            spread.reshape(-1, channels),
            point_weights[layer_index],
            preferred_element_type=jnp.float32,
        )
        current = current + mixed.reshape(current.shape)
    projected = jnp.dot(
        current.astype(jnp.bfloat16).reshape(-1, channels),
        project_weight,
        preferred_element_type=jnp.float32,
    )
    mismatch = (projected - target.astype(jnp.float32).reshape(projected.shape)).astype(
        jnp.bfloat16
    )
    gradient = lax.dot_general(
        mismatch, project_weight, (((1,), (1,)), ((), ())), preferred_element_type=jnp.float32
    ).reshape(current.shape)
    for layer_index in reversed(range(depth_weights.shape[0])):
        backward = lax.dot_general(
            gradient.astype(jnp.bfloat16).reshape(-1, channels),
            point_weights[layer_index],
            (((1,), (1,)), ((), ())),
            preferred_element_type=jnp.float32,
        )
        backward = backward.astype(jnp.bfloat16).reshape(current.shape)
        flipped = depth_weights[layer_index][::-1, ::-1, ::-1]
        spread_back = depthwise(extend_future(backward), flipped)
        gradient = gradient + spread_back * silu_slope(stored[layer_index])
    return gradient.astype(jnp.bfloat16)


def on_device(
    teacher_in, teacher_weights, student_in, depth_weights, point_weights, project_weight
):
    target = teacher_in
    current = target.astype(jnp.float32)
    active = jax.nn.silu(root_norm(current)).astype(jnp.bfloat16)
    middle = dense_conv(teacher_extend(active), teacher_weights[0, 0])
    second = jax.nn.silu(root_norm(middle)).astype(jnp.bfloat16)
    target = (current + dense_conv(teacher_extend(second), teacher_weights[0, 1])).astype(
        jnp.bfloat16
    )
    regrouped = lax.all_to_all(target, "wa", split_axis=1, concat_axis=2, tiled=True)
    return student_pass(
        student_in,
        regrouped,
        depth_weights,
        point_weights,
        project_weight,
        rows_extend_past,
        rows_extend_future,
    )


def solution(mesh):
    placed = (P("ta", "ha", "wa", None), P(), P("ta", ("ha", "wa"), None, None), P(), P(), P())
    return jax.shard_map(
        on_device,
        mesh=mesh,
        in_specs=placed,
        out_specs=P("ta", ("ha", "wa"), None, None),
        check_vma=False,
    )
```

profile of v0, /device:TPU:32, one launch (start us, length us, event | category | flops | bytes accessed | tf_op | source)
XLA Modules:
  0.0 256.7 jit_solution(6268636678672001673)
XLA Ops:
  2.3 3.4 %collective-permute-start.12 = (bf16[2,32,8,192]{3,2,1,0:T(8,128)(2,1)S(1)}, bf16[2,32,8,192]{3,2,1,0:T(8,128)(2,1)S(1)}, u32[]{:S(2)}, u32[]{:S(2)}) collective-permute-start(bf16[2,32,8,192]{3,2,1,0:T(8,128)(2,1)S(1)} %fusion.17), channel_id=1, source_target_pairs={{0,128},{128,256},{256,384},{1,129},{129,257},{257,385},{2,130},{1... | collective-permute-start | bytes 589832 | tf_op jit(solution)/shard_map/ppermute | solution.py:10
  6.7 3.4 %collective-permute-start = (bf16[2,1,256,128]{3,2,0,1:T(8,128)(2,1)S(1)}, bf16[2,1,256,128]{3,2,0,1:T(8,128)(2,1)S(1)}, u32[]{:S(2)}, u32[]{:S(2)}) collective-permute-start(bf16[2,1,256,128]{3,2,0,1:T(8,128)(2,1)S(1)} %fusion.22), channel_id=1, source_target_pairs={{0,128},{128,256},{256,384},{1,129},{129,257},{257,385},{2,130},{1... | collective-permute-start | bytes 393224 | tf_op jit(solution)/shard_map/ppermute | solution.py:10
  13.7 4.6 %fusion.65 = (bf16[1,1,3,3,3,192,192]{6,5,4,3,2,1,0:T(8,128)(2,1)S(1)}, bf16[1,1,3,3,3,192,192]{6,5,4,3,2,1,0:T(8,128)(2,1)}) fusion(bf16[1,2,3,3,3,192,192]{6,5,4,3,2,1,0:T(8,128)(2,1)} %param.7), kind=kLoop, calls=%fused_computation.280 | loop fusion | bytes 7962624 | tf_op jit(solution)/shard_map/slice | solution.py:143
  20.3 9.7 %collective-permute-start.2 = (bf16[4,1,256,128]{3,2,0,1:T(8,128)(2,1)}, bf16[4,1,256,128]{3,2,0,1:T(8,128)(2,1)}, u32[]{:S(2)}, u32[]{:S(2)}) collective-permute-start(bf16[4,1,256,128]{3,2,0,1:T(8,128)(2,1)} %pad_maximum_fusion.4), channel_id=1, source_target_pairs={{1,0},{2,1},{3,2},{4,3},{5,4},{6,5},{7,6},{8,7},{9,8},{10,9},{11,1... | collective-permute-start | bytes 786440 | tf_op jit(solution)/shard_map/ppermute | solution.py:21
  34.2 4.5 %collective-permute-start.13 = (bf16[4,1,8,192]{3,2,1,0:T(8,128)(2,1)S(1)}, bf16[4,1,8,192]{3,2,1,0:T(8,128)(2,1)S(1)}, u32[]{:S(2)}, u32[]{:S(2)}) collective-permute-start(bf16[4,1,8,192]{3,2,1,0:T(8,128)(2,1)S(1)} %get-tuple-element.75), channel_id=1, source_target_pairs={{0,32},{32,64},{64,96},{1,33},{33,65},{65,97},{2,34},{34,66},{66,9... | collective-permute-start | bytes 36872 | tf_op jit(solution)/shard_map/ppermute | solution.py:18
  39.4 2.5 collective-permute-done.13
  43.4 3.0 %collective-permute-start.15 = (bf16[4,34,1,192]{3,2,1,0:T(2,128)(2,1)S(1)}, bf16[4,34,1,192]{3,2,1,0:T(2,128)(2,1)S(1)}, u32[]{:S(2)}, u32[]{:S(2)}) collective-permute-start(bf16[4,34,1,192]{3,2,1,0:T(2,128)(2,1)S(1)} %get-tuple-element.56), channel_id=1, source_target_pairs={{0,1},{1,2},{2,3},{3,4},{4,5},{5,6},{6,7},{7,8},{8,9},{9,10},{10,1... | collective-permute-start | bytes 156680 | tf_op jit(solution)/shard_map/ppermute | solution.py:18
  50.9 10.1 %concatenate.146 = bf16[2,32,8,5184]{3,2,1,0:T(8,128)(2,1)} concatenate(bf16[2,32,8,192]{3,2,1,0:T(8,128)(2,1)} %get-tuple-element.197, bf16[2,32,8,192]{3,2,1,0:T(8,128)(2,1)} %get-tuple-element.206, bf16[2,32,8,192]{3,2,1,0:T(8,128)(2,1)} %get-tuple-element.39, bf16[2,32,8,192]{3,2,1,0:T(8,128)(2,1)} %get-tuple-element.198, ...), dimensions={3} | concatenate | bytes 10616832 | tf_op jit(solution)/shard_map/concatenate | solution.py:51
  61.0 5.0 %multiply_reduce_fusion = (f32[2,32,8]{2,1,0:T(8,128)S(1)}, f32[2,32,8,192]{3,2,1,0:T(8,128)S(1)}) fusion(bf16[2,32,8,5184]{3,2,1,0:T(8,128)(2,1)} %concatenate.146, bf16[5184,192,1,1]{1,0,3,2:T(8,128)(2,1)} %bitcast.325), kind=kOutput, calls=%fused_computation.65 | convolution fusion | flops 1019411968 | bytes 7694336 | tf_op jit(solution)/shard_map/dot_general | solution.py:52
  66.6 3.1 %collective-permute-start.17 = (bf16[2,32,8,192]{3,2,1,0:T(8,128)(2,1)S(1)}, bf16[2,32,8,192]{3,2,1,0:T(8,128)(2,1)S(1)}, u32[]{:S(2)}, u32[]{:S(2)}) collective-permute-start(bf16[2,32,8,192]{3,2,1,0:T(8,128)(2,1)S(1)} %multiply_convert_fusion), channel_id=1, source_target_pairs={{0,128},{128,256},{256,384},{1,129},{129,257},{257,385},{2,130},{1... | collective-permute-start | bytes 589832 | tf_op jit(solution)/shard_map/ppermute | solution.py:10
  77.9 4.8 %collective-permute-start.18 = (bf16[4,1,8,192]{3,2,1,0:T(8,128)(2,1)S(1)}, bf16[4,1,8,192]{3,2,1,0:T(8,128)(2,1)S(1)}, u32[]{:S(2)}, u32[]{:S(2)}) collective-permute-start(bf16[4,1,8,192]{3,2,1,0:T(8,128)(2,1)S(1)} %get-tuple-element.71), channel_id=1, source_target_pairs={{0,32},{32,64},{64,96},{1,33},{33,65},{65,97},{2,34},{34,66},{66,9... | collective-permute-start | bytes 36872 | tf_op jit(solution)/shard_map/ppermute | solution.py:18
  82.8 2.9 %collective-permute-done.18 = bf16[4,1,8,192]{3,2,1,0:T(8,128)(2,1)S(1)} collective-permute-done((bf16[4,1,8,192]{3,2,1,0:T(8,128)(2,1)S(1)}, bf16[4,1,8,192]{3,2,1,0:T(8,128)(2,1)S(1)}, u32[]{:S(2)}, u32[]{:S(2)}) %collective-permute-start.18) | collective-permute-done | bytes 12320 | tf_op jit(solution)/shard_map/ppermute | solution.py:18
  87.2 3.0 %collective-permute-start.20 = (bf16[4,34,1,192]{3,2,1,0:T(2,128)(2,1)S(1)}, bf16[4,34,1,192]{3,2,1,0:T(2,128)(2,1)S(1)}, u32[]{:S(2)}, u32[]{:S(2)}) collective-permute-start(bf16[4,34,1,192]{3,2,1,0:T(2,128)(2,1)S(1)} %get-tuple-element.52), channel_id=1, source_target_pairs={{0,1},{1,2},{2,3},{3,4},{4,5},{5,6},{6,7},{7,8},{8,9},{9,10},{10,1... | collective-permute-start | bytes 156680 | tf_op jit(solution)/shard_map/ppermute | solution.py:18
  91.4 4.3 %collective-permute-start.5 = (bf16[4,1,256,128]{3,2,0,1:T(8,128)(2,1)S(1)}, bf16[4,1,256,128]{3,2,0,1:T(8,128)(2,1)S(1)}, u32[]{:S(2)}, u32[]{:S(2)}) collective-permute-start(bf16[4,1,256,128]{3,2,0,1:T(8,128)(2,1)S(1)} %pad_maximum_fusion.5), channel_id=1, source_target_pairs={{1,0},{2,1},{3,2},{4,3},{5,4},{6,5},{7,6},{8,7},{9,8},{10,9},{11,1... | collective-permute-start | bytes 786440 | tf_op jit(solution)/shard_map/ppermute | solution.py:21
  99.7 7.1 %collective-permute-done.4 = bf16[4,1,256,128]{3,2,0,1:T(8,128)(2,1)S(1)} collective-permute-done((bf16[4,1,256,128]{3,2,0,1:T(8,128)(2,1)S(1)}, bf16[4,1,256,128]{3,2,0,1:T(8,128)(2,1)S(1)}, u32[]{:S(2)}, u32[]{:S(2)}) %collective-permute-start.4) | collective-permute-done | bytes 262176 | tf_op jit(solution)/shard_map/ppermute | solution.py:18
  109.0 2.6 %collective-permute-start.6 = (bf16[2,1,256,128]{3,2,0,1:T(8,128)(2,1)S(1)}, bf16[2,1,256,128]{3,2,0,1:T(8,128)(2,1)S(1)}, u32[]{:S(2)}, u32[]{:S(2)}) collective-permute-start(bf16[2,1,256,128]{3,2,0,1:T(8,128)(2,1)S(1)} %get-tuple-element.193), channel_id=1, source_target_pairs={{0,128},{128,256},{256,384},{1,129},{129,257},{257,385},{2,130},{1... | collective-permute-start | bytes 393224 | tf_op jit(solution)/shard_map/ppermute | solution.py:10
  116.9 2.6 %collective-permute-start.7 = (bf16[4,1,256,128]{3,2,0,1:T(8,128)(2,1)}, bf16[4,1,256,128]{3,2,0,1:T(8,128)(2,1)}, u32[]{:S(2)}, u32[]{:S(2)}) collective-permute-start(bf16[4,1,256,128]{3,2,0,1:T(8,128)(2,1)} %pad_maximum_fusion.6), channel_id=1, source_target_pairs={{0,1},{1,2},{2,3},{3,4},{4,5},{5,6},{6,7},{7,8},{8,9},{9,10},{10,1... | collective-permute-start | bytes 786440 | tf_op jit(solution)/shard_map/ppermute | solution.py:18
  121.0 10.0 %concatenate.153 = bf16[2,32,8,5184]{3,2,1,0:T(8,128)(2,1)} concatenate(bf16[2,32,8,192]{3,2,1,0:T(8,128)(2,1)} %get-tuple-element.30, bf16[2,32,8,192]{3,2,1,0:T(8,128)(2,1)} %get-tuple-element.62, bf16[2,32,8,192]{3,2,1,0:T(8,128)(2,1)} %get-tuple-element.21, bf16[2,32,8,192]{3,2,1,0:T(8,128)(2,1)} %get-tuple-element.29, bf16[2,32,8,192]{3,2,1,0:T(8,128)(2,1)S(1)} %collective-permute-done.17, ...), dimensions={3} | concatenate | bytes 10616832 | tf_op jit(solution)/shard_map/concatenate | solution.py:51
  133.0 2.5 multiply_convert_fusion.1
  135.5 4.4 %collective-permute-start.9 = (bf16[2,1,256,128]{3,2,0,1:T(8,128)(2,1)S(1)}, bf16[2,1,256,128]{3,2,0,1:T(8,128)(2,1)S(1)}, u32[]{:S(2)}, u32[]{:S(2)}) collective-permute-start(bf16[2,1,256,128]{3,2,0,1:T(8,128)(2,1)S(1)} %get-tuple-element.195), channel_id=1, source_target_pairs={{0,128},{128,256},{256,384},{1,129},{129,257},{257,385},{2,130},{1... | collective-permute-start | bytes 393224 | tf_op jit(solution)/shard_map/ppermute | solution.py:10
  142.2 10.8 %all-to-all-start = ((bf16[2,32,8,192]{3,2,0,1:T(8,128)(2,1)}), bf16[2,32,8,192]{3,2,0,1:T(8,128)(2,1)S(1)}, u32[]{:S(2)}, u32[]{:S(2)}) async-start(bf16[2,32,8,192]{3,2,0,1:T(8,128)(2,1)} %copy.24), calls=%async_computation | async-start | bytes 524288 | tf_op jit(solution)/shard_map/all_to_all | solution.py:146
  153.1 3.9 %collective-permute-start.11 = (bf16[4,1,256,128]{3,2,0,1:T(8,128)(2,1)S(1)}, bf16[4,1,256,128]{3,2,0,1:T(8,128)(2,1)S(1)}, u32[]{:S(2)}, u32[]{:S(2)}) collective-permute-start(bf16[4,1,256,128]{3,2,0,1:T(8,128)(2,1)S(1)} %pad_maximum_fusion.7), channel_id=1, source_target_pairs={{1,0},{2,1},{3,2},{4,3},{5,4},{6,5},{7,6},{8,7},{9,8},{10,9},{11,1... | collective-permute-start | bytes 786440 | tf_op jit(solution)/shard_map/ppermute | solution.py:21
  159.0 6.3 %all-to-all-done = bf16[2,32,8,192]{3,2,0,1:T(8,128)(2,1)S(1)} async-done(((bf16[2,32,8,192]{3,2,0,1:T(8,128)(2,1)}), bf16[2,32,8,192]{3,2,0,1:T(8,128)(2,1)S(1)}, u32[]{:S(2)}, u32[]{:S(2)}) %all-to-all-start) | async-done | bytes 196640 | tf_op jit(solution)/shard_map/all_to_all | solution.py:146
  165.6 2.5 collective-permute-done.10
  171.4 5.6 %collective-permute-done.22 = bf16[2,1,256,128]{3,2,0,1:T(8,128)(2,1)S(1)} collective-permute-done((bf16[2,1,256,128]{3,2,0,1:T(8,128)(2,1)S(1)}, bf16[2,1,256,128]{3,2,0,1:T(8,128)(2,1)S(1)}, u32[]{:S(2)}, u32[]{:S(2)}) %collective-permute-start.22) | collective-permute-done | bytes 131104 | tf_op jit(solution)/shard_map/ppermute | solution.py:10
  182.8 7.1 %collective-permute-done.23 = bf16[4,1,256,128]{3,2,0,1:T(8,128)(2,1)S(1)} collective-permute-done((bf16[4,1,256,128]{3,2,0,1:T(8,128)(2,1)S(1)}, bf16[4,1,256,128]{3,2,0,1:T(8,128)(2,1)S(1)}, u32[]{:S(2)}, u32[]{:S(2)}) %collective-permute-start.23) | collective-permute-done | bytes 262176 | tf_op jit(solution)/shard_map/ppermute | solution.py:18
  192.8 5.6 %collective-permute-done.25 = bf16[2,1,256,128]{3,2,0,1:T(8,128)(2,1)S(1)} collective-permute-done((bf16[2,1,256,128]{3,2,0,1:T(8,128)(2,1)S(1)}, bf16[2,1,256,128]{3,2,0,1:T(8,128)(2,1)S(1)}, u32[]{:S(2)}, u32[]{:S(2)}) %collective-permute-start.25) | collective-permute-done | bytes 131104 | tf_op jit(solution)/shard_map/ppermute | solution.py:10
  204.2 7.1 %collective-permute-done.26 = bf16[4,1,256,128]{3,2,0,1:T(8,128)(2,1)S(1)} collective-permute-done((bf16[4,1,256,128]{3,2,0,1:T(8,128)(2,1)S(1)}, bf16[4,1,256,128]{3,2,0,1:T(8,128)(2,1)S(1)}, u32[]{:S(2)}, u32[]{:S(2)}) %collective-permute-start.26) | collective-permute-done | bytes 262176 | tf_op jit(solution)/shard_map/ppermute | solution.py:18
  214.4 5.6 %collective-permute-done.28 = bf16[2,1,256,128]{3,2,0,1:T(8,128)(2,1)S(1)} collective-permute-done((bf16[2,1,256,128]{3,2,0,1:T(8,128)(2,1)S(1)}, bf16[2,1,256,128]{3,2,0,1:T(8,128)(2,1)S(1)}, u32[]{:S(2)}, u32[]{:S(2)}) %collective-permute-start.28) | collective-permute-done | bytes 131104 | tf_op jit(solution)/shard_map/ppermute | solution.py:10
  225.8 7.1 %collective-permute-done.29 = bf16[4,1,256,128]{3,2,0,1:T(8,128)(2,1)S(1)} collective-permute-done((bf16[4,1,256,128]{3,2,0,1:T(8,128)(2,1)S(1)}, bf16[4,1,256,128]{3,2,0,1:T(8,128)(2,1)S(1)}, u32[]{:S(2)}, u32[]{:S(2)}) %collective-permute-start.29) | collective-permute-done | bytes 262176 | tf_op jit(solution)/shard_map/ppermute | solution.py:18
  236.0 5.6 %collective-permute-done.31 = bf16[2,1,256,128]{3,2,0,1:T(8,128)(2,1)S(1)} collective-permute-done((bf16[2,1,256,128]{3,2,0,1:T(8,128)(2,1)S(1)}, bf16[2,1,256,128]{3,2,0,1:T(8,128)(2,1)S(1)}, u32[]{:S(2)}, u32[]{:S(2)}) %collective-permute-start.31) | collective-permute-done | bytes 131104 | tf_op jit(solution)/shard_map/ppermute | solution.py:10
  247.4 7.1 %collective-permute-done.32 = bf16[4,1,256,128]{3,2,0,1:T(8,128)(2,1)S(1)} collective-permute-done((bf16[4,1,256,128]{3,2,0,1:T(8,128)(2,1)S(1)}, bf16[4,1,256,128]{3,2,0,1:T(8,128)(2,1)S(1)}, u32[]{:S(2)}, u32[]{:S(2)}) %collective-permute-start.32) | collective-permute-done | bytes 262176 | tf_op jit(solution)/shard_map/ppermute | solution.py:18
  (416 shorter events, 85.8 us)
Async XLA Ops:
  2.3 29.6 %collective-permute-start.12 = (bf16[2,32,8,192]{3,2,1,0:T(8,128)(2,1)S(1)}, bf16[2,32,8,192]{3,2,1,0:T(8,128)(2,1)S(1)}, u32[]{:S(2)}, u32[]{:S(2)}) collective-permute-start(bf16[2,32,8,192]{3,2,1,0:T(8,128)(2,1)S(1)} %fusion.17), channel_id=1, source_target_pairs={{0,128},{128,256},{256,384},{1,129},{129,257},{257,385},{2,130},{1... | collective-permute-start | bytes 589832 | tf_op jit(solution)/shard_map/ppermute | solution.py:10
  6.7 12.8 %collective-permute-start = (bf16[2,1,256,128]{3,2,0,1:T(8,128)(2,1)S(1)}, bf16[2,1,256,128]{3,2,0,1:T(8,128)(2,1)S(1)}, u32[]{:S(2)}, u32[]{:S(2)}) collective-permute-start(bf16[2,1,256,128]{3,2,0,1:T(8,128)(2,1)S(1)} %fusion.22), channel_id=1, source_target_pairs={{0,128},{128,256},{256,384},{1,129},{129,257},{257,385},{2,130},{1... | collective-permute-start | bytes 393224 | tf_op jit(solution)/shard_map/ppermute | solution.py:10
  20.3 49.5 %collective-permute-start.2 = (bf16[4,1,256,128]{3,2,0,1:T(8,128)(2,1)}, bf16[4,1,256,128]{3,2,0,1:T(8,128)(2,1)}, u32[]{:S(2)}, u32[]{:S(2)}) collective-permute-start(bf16[4,1,256,128]{3,2,0,1:T(8,128)(2,1)} %pad_maximum_fusion.4), channel_id=1, source_target_pairs={{1,0},{2,1},{3,2},{4,3},{5,4},{6,5},{7,6},{8,7},{9,8},{10,9},{11,1... | collective-permute-start | bytes 786440 | tf_op jit(solution)/shard_map/ppermute | solution.py:21
  30.0 39.8 %collective-permute-start.1 = (bf16[4,1,256,128]{3,2,0,1:T(8,128)(2,1)}, bf16[4,1,256,128]{3,2,0,1:T(8,128)(2,1)}, u32[]{:S(2)}, u32[]{:S(2)}) collective-permute-start(bf16[4,1,256,128]{3,2,0,1:T(8,128)(2,1)} %pad_maximum_fusion.4), channel_id=1, source_target_pairs={{0,1},{1,2},{2,3},{3,4},{4,5},{5,6},{6,7},{7,8},{8,9},{9,10},{10,1... | collective-permute-start | bytes 786440 | tf_op jit(solution)/shard_map/ppermute | solution.py:18
  31.9 7.5 %collective-permute-start.14 = (bf16[4,1,8,192]{3,2,1,0:T(8,128)(2,1)S(1)}, bf16[4,1,8,192]{3,2,1,0:T(8,128)(2,1)S(1)}, u32[]{:S(2)}, u32[]{:S(2)}) collective-permute-start(bf16[4,1,8,192]{3,2,1,0:T(8,128)(2,1)S(1)} %get-tuple-element.76), channel_id=1, source_target_pairs={{32,0},{64,32},{96,64},{33,1},{65,33},{97,65},{34,2},{66,34},{98,6... | collective-permute-start | bytes 36872 | tf_op jit(solution)/shard_map/ppermute | solution.py:21
  34.2 7.7 %collective-permute-start.13 = (bf16[4,1,8,192]{3,2,1,0:T(8,128)(2,1)S(1)}, bf16[4,1,8,192]{3,2,1,0:T(8,128)(2,1)S(1)}, u32[]{:S(2)}, u32[]{:S(2)}) collective-permute-start(bf16[4,1,8,192]{3,2,1,0:T(8,128)(2,1)S(1)} %get-tuple-element.75), channel_id=1, source_target_pairs={{0,32},{32,64},{64,96},{1,33},{33,65},{65,97},{2,34},{34,66},{66,9... | collective-permute-start | bytes 36872 | tf_op jit(solution)/shard_map/ppermute | solution.py:18
  66.6 9.4 %collective-permute-start.17 = (bf16[2,32,8,192]{3,2,1,0:T(8,128)(2,1)S(1)}, bf16[2,32,8,192]{3,2,1,0:T(8,128)(2,1)S(1)}, u32[]{:S(2)}, u32[]{:S(2)}) collective-permute-start(bf16[2,32,8,192]{3,2,1,0:T(8,128)(2,1)S(1)} %multiply_convert_fusion), channel_id=1, source_target_pairs={{0,128},{128,256},{256,384},{1,129},{129,257},{257,385},{2,130},{1... | collective-permute-start | bytes 589832 | tf_op jit(solution)/shard_map/ppermute | solution.py:10
  73.7 17.7 %collective-permute-start.3 = (bf16[2,1,256,128]{3,2,0,1:T(8,128)(2,1)S(1)}, bf16[2,1,256,128]{3,2,0,1:T(8,128)(2,1)S(1)}, u32[]{:S(2)}, u32[]{:S(2)}) collective-permute-start(bf16[2,1,256,128]{3,2,0,1:T(8,128)(2,1)S(1)} %get-tuple-element.191), channel_id=1, source_target_pairs={{0,128},{128,256},{256,384},{1,129},{129,257},{257,385},{2,130},{1... | collective-permute-start | bytes 393224 | tf_op jit(solution)/shard_map/ppermute | solution.py:10
  76.0 6.8 %collective-permute-start.19 = (bf16[4,1,8,192]{3,2,1,0:T(8,128)(2,1)S(1)}, bf16[4,1,8,192]{3,2,1,0:T(8,128)(2,1)S(1)}, u32[]{:S(2)}, u32[]{:S(2)}) collective-permute-start(bf16[4,1,8,192]{3,2,1,0:T(8,128)(2,1)S(1)} %get-tuple-element.72), channel_id=1, source_target_pairs={{32,0},{64,32},{96,64},{33,1},{65,33},{97,65},{34,2},{66,34},{98,6... | collective-permute-start | bytes 36872 | tf_op jit(solution)/shard_map/ppermute | solution.py:21
  77.9 7.7 %collective-permute-start.18 = (bf16[4,1,8,192]{3,2,1,0:T(8,128)(2,1)S(1)}, bf16[4,1,8,192]{3,2,1,0:T(8,128)(2,1)S(1)}, u32[]{:S(2)}, u32[]{:S(2)}) collective-permute-start(bf16[4,1,8,192]{3,2,1,0:T(8,128)(2,1)S(1)} %get-tuple-element.71), channel_id=1, source_target_pairs={{0,32},{32,64},{64,96},{1,33},{33,65},{65,97},{2,34},{34,66},{66,9... | collective-permute-start | bytes 36872 | tf_op jit(solution)/shard_map/ppermute | solution.py:18
  85.9 12.9 %collective-permute-start.21 = (bf16[4,34,1,192]{3,2,1,0:T(2,128)(2,1)S(1)}, bf16[4,34,1,192]{3,2,1,0:T(2,128)(2,1)S(1)}, u32[]{:S(2)}, u32[]{:S(2)}) collective-permute-start(bf16[4,34,1,192]{3,2,1,0:T(2,128)(2,1)S(1)} %get-tuple-element.51), channel_id=1, source_target_pairs={{1,0},{2,1},{3,2},{4,3},{5,4},{6,5},{7,6},{8,7},{9,8},{10,9},{11,1... | collective-permute-start | bytes 156680 | tf_op jit(solution)/shard_map/ppermute | solution.py:21
  87.2 11.6 %collective-permute-start.20 = (bf16[4,34,1,192]{3,2,1,0:T(2,128)(2,1)S(1)}, bf16[4,34,1,192]{3,2,1,0:T(2,128)(2,1)S(1)}, u32[]{:S(2)}, u32[]{:S(2)}) collective-permute-start(bf16[4,34,1,192]{3,2,1,0:T(2,128)(2,1)S(1)} %get-tuple-element.52), channel_id=1, source_target_pairs={{0,1},{1,2},{2,3},{3,4},{4,5},{5,6},{6,7},{7,8},{8,9},{9,10},{10,1... | collective-permute-start | bytes 156680 | tf_op jit(solution)/shard_map/ppermute | solution.py:18
  91.4 8.2 %collective-permute-start.5 = (bf16[4,1,256,128]{3,2,0,1:T(8,128)(2,1)S(1)}, bf16[4,1,256,128]{3,2,0,1:T(8,128)(2,1)S(1)}, u32[]{:S(2)}, u32[]{:S(2)}) collective-permute-start(bf16[4,1,256,128]{3,2,0,1:T(8,128)(2,1)S(1)} %pad_maximum_fusion.5), channel_id=1, source_target_pairs={{1,0},{2,1},{3,2},{4,3},{5,4},{6,5},{7,6},{8,7},{9,8},{10,9},{11,1... | collective-permute-start | bytes 786440 | tf_op jit(solution)/shard_map/ppermute | solution.py:21
  95.7 11.0 %collective-permute-start.4 = (bf16[4,1,256,128]{3,2,0,1:T(8,128)(2,1)S(1)}, bf16[4,1,256,128]{3,2,0,1:T(8,128)(2,1)S(1)}, u32[]{:S(2)}, u32[]{:S(2)}) collective-permute-start(bf16[4,1,256,128]{3,2,0,1:T(8,128)(2,1)S(1)} %pad_maximum_fusion.5), channel_id=1, source_target_pairs={{0,1},{1,2},{2,3},{3,4},{4,5},{5,6},{6,7},{7,8},{8,9},{9,10},{10,1... | collective-permute-start | bytes 786440 | tf_op jit(solution)/shard_map/ppermute | solution.py:18
  114.9 16.3 %collective-permute-start.8 = (bf16[4,1,256,128]{3,2,0,1:T(8,128)(2,1)}, bf16[4,1,256,128]{3,2,0,1:T(8,128)(2,1)}, u32[]{:S(2)}, u32[]{:S(2)}) collective-permute-start(bf16[4,1,256,128]{3,2,0,1:T(8,128)(2,1)} %pad_maximum_fusion.6), channel_id=1, source_target_pairs={{1,0},{2,1},{3,2},{4,3},{5,4},{6,5},{7,6},{8,7},{9,8},{10,9},{11,1... | collective-permute-start | bytes 786440 | tf_op jit(solution)/shard_map/ppermute | solution.py:21
  116.9 14.4 %collective-permute-start.7 = (bf16[4,1,256,128]{3,2,0,1:T(8,128)(2,1)}, bf16[4,1,256,128]{3,2,0,1:T(8,128)(2,1)}, u32[]{:S(2)}, u32[]{:S(2)}) collective-permute-start(bf16[4,1,256,128]{3,2,0,1:T(8,128)(2,1)} %pad_maximum_fusion.6), channel_id=1, source_target_pairs={{0,1},{1,2},{2,3},{3,4},{4,5},{5,6},{6,7},{7,8},{8,9},{9,10},{10,1... | collective-permute-start | bytes 786440 | tf_op jit(solution)/shard_map/ppermute | solution.py:18
  135.5 17.6 %collective-permute-start.9 = (bf16[2,1,256,128]{3,2,0,1:T(8,128)(2,1)S(1)}, bf16[2,1,256,128]{3,2,0,1:T(8,128)(2,1)S(1)}, u32[]{:S(2)}, u32[]{:S(2)}) collective-permute-start(bf16[2,1,256,128]{3,2,0,1:T(8,128)(2,1)S(1)} %get-tuple-element.195), channel_id=1, source_target_pairs={{0,128},{128,256},{256,384},{1,129},{129,257},{257,385},{2,130},{1... | collective-permute-start | bytes 393224 | tf_op jit(solution)/shard_map/ppermute | solution.py:10
  142.2 23.1 %all-to-all-start = ((bf16[2,32,8,192]{3,2,0,1:T(8,128)(2,1)}), bf16[2,32,8,192]{3,2,0,1:T(8,128)(2,1)S(1)}, u32[]{:S(2)}, u32[]{:S(2)}) async-start(bf16[2,32,8,192]{3,2,0,1:T(8,128)(2,1)} %copy.24), calls=%async_computation | async-start | bytes 524288 | tf_op jit(solution)/shard_map/all_to_all | solution.py:146
  153.1 12.4 %collective-permute-start.11 = (bf16[4,1,256,128]{3,2,0,1:T(8,128)(2,1)S(1)}, bf16[4,1,256,128]{3,2,0,1:T(8,128)(2,1)S(1)}, u32[]{:S(2)}, u32[]{:S(2)}) collective-permute-start(bf16[4,1,256,128]{3,2,0,1:T(8,128)(2,1)S(1)} %pad_maximum_fusion.7), channel_id=1, source_target_pairs={{1,0},{2,1},{3,2},{4,3},{5,4},{6,5},{7,6},{8,7},{9,8},{10,9},{11,1... | collective-permute-start | bytes 786440 | tf_op jit(solution)/shard_map/ppermute | solution.py:21
  157.0 11.1 %collective-permute-start.10 = (bf16[4,1,256,128]{3,2,0,1:T(8,128)(2,1)S(1)}, bf16[4,1,256,128]{3,2,0,1:T(8,128)(2,1)S(1)}, u32[]{:S(2)}, u32[]{:S(2)}) collective-permute-start(bf16[4,1,256,128]{3,2,0,1:T(8,128)(2,1)S(1)} %pad_maximum_fusion.7), channel_id=1, source_target_pairs={{0,1},{1,2},{2,3},{3,4},{4,5},{5,6},{6,7},{7,8},{8,9},{9,10},{10,1... | collective-permute-start | bytes 786440 | tf_op jit(solution)/shard_map/ppermute | solution.py:18
  170.1 6.9 %collective-permute-start.22 = (bf16[2,1,256,128]{3,2,0,1:T(8,128)(2,1)S(1)}, bf16[2,1,256,128]{3,2,0,1:T(8,128)(2,1)S(1)}, u32[]{:S(2)}, u32[]{:S(2)}) collective-permute-start(bf16[2,1,256,128]{3,2,0,1:T(8,128)(2,1)S(1)} %bitcast.336), channel_id=1, source_target_pairs={{128,0},{256,128},{384,256},{129,1},{257,129},{385,257},{130,2},{2... | collective-permute-start | bytes 393224 | tf_op jit(solution)/shard_map/ppermute | solution.py:10
  177.0 5.8 %collective-permute-start.24 = (bf16[4,1,256,128]{3,2,0,1:T(8,128)(2,1)S(1)}, bf16[4,1,256,128]{3,2,0,1:T(8,128)(2,1)S(1)}, u32[]{:S(2)}, u32[]{:S(2)}) collective-permute-start(bf16[4,1,256,128]{3,2,0,1:T(8,128)(2,1)S(1)} %pad_maximum_fusion.8), channel_id=1, source_target_pairs={{1,0},{2,1},{3,2},{4,3},{5,4},{6,5},{7,6},{8,7},{9,8},{10,9},{11,1... | collective-permute-start | bytes 786440 | tf_op jit(solution)/shard_map/ppermute | solution.py:21
  178.9 11.0 %collective-permute-start.23 = (bf16[4,1,256,128]{3,2,0,1:T(8,128)(2,1)S(1)}, bf16[4,1,256,128]{3,2,0,1:T(8,128)(2,1)S(1)}, u32[]{:S(2)}, u32[]{:S(2)}) collective-permute-start(bf16[4,1,256,128]{3,2,0,1:T(8,128)(2,1)S(1)} %pad_maximum_fusion.8), channel_id=1, source_target_pairs={{0,1},{1,2},{2,3},{3,4},{4,5},{5,6},{6,7},{7,8},{8,9},{9,10},{10,1... | collective-permute-start | bytes 786440 | tf_op jit(solution)/shard_map/ppermute | solution.py:18
  191.5 6.9 %collective-permute-start.25 = (bf16[2,1,256,128]{3,2,0,1:T(8,128)(2,1)S(1)}, bf16[2,1,256,128]{3,2,0,1:T(8,128)(2,1)S(1)}, u32[]{:S(2)}, u32[]{:S(2)}) collective-permute-start(bf16[2,1,256,128]{3,2,0,1:T(8,128)(2,1)S(1)} %bitcast.328), channel_id=1, source_target_pairs={{128,0},{256,128},{384,256},{129,1},{257,129},{385,257},{130,2},{2... | collective-permute-start | bytes 393224 | tf_op jit(solution)/shard_map/ppermute | solution.py:10
  198.4 5.8 %collective-permute-start.27 = (bf16[4,1,256,128]{3,2,0,1:T(8,128)(2,1)S(1)}, bf16[4,1,256,128]{3,2,0,1:T(8,128)(2,1)S(1)}, u32[]{:S(2)}, u32[]{:S(2)}) collective-permute-start(bf16[4,1,256,128]{3,2,0,1:T(8,128)(2,1)S(1)} %pad_maximum_fusion.9), channel_id=1, source_target_pairs={{1,0},{2,1},{3,2},{4,3},{5,4},{6,5},{7,6},{8,7},{9,8},{10,9},{11,1... | collective-permute-start | bytes 786440 | tf_op jit(solution)/shard_map/ppermute | solution.py:21
  200.3 11.0 %collective-permute-start.26 = (bf16[4,1,256,128]{3,2,0,1:T(8,128)(2,1)S(1)}, bf16[4,1,256,128]{3,2,0,1:T(8,128)(2,1)S(1)}, u32[]{:S(2)}, u32[]{:S(2)}) collective-permute-start(bf16[4,1,256,128]{3,2,0,1:T(8,128)(2,1)S(1)} %pad_maximum_fusion.9), channel_id=1, source_target_pairs={{0,1},{1,2},{2,3},{3,4},{4,5},{5,6},{6,7},{7,8},{8,9},{9,10},{10,1... | collective-permute-start | bytes 786440 | tf_op jit(solution)/shard_map/ppermute | solution.py:18
  213.1 6.9 %collective-permute-start.28 = (bf16[2,1,256,128]{3,2,0,1:T(8,128)(2,1)S(1)}, bf16[2,1,256,128]{3,2,0,1:T(8,128)(2,1)S(1)}, u32[]{:S(2)}, u32[]{:S(2)}) collective-permute-start(bf16[2,1,256,128]{3,2,0,1:T(8,128)(2,1)S(1)} %bitcast.332), channel_id=1, source_target_pairs={{128,0},{256,128},{384,256},{129,1},{257,129},{385,257},{130,2},{2... | collective-permute-start | bytes 393224 | tf_op jit(solution)/shard_map/ppermute | solution.py:10
  220.0 5.8 %collective-permute-start.30 = (bf16[4,1,256,128]{3,2,0,1:T(8,128)(2,1)S(1)}, bf16[4,1,256,128]{3,2,0,1:T(8,128)(2,1)S(1)}, u32[]{:S(2)}, u32[]{:S(2)}) collective-permute-start(bf16[4,1,256,128]{3,2,0,1:T(8,128)(2,1)S(1)} %pad_maximum_fusion.10), channel_id=1, source_target_pairs={{1,0},{2,1},{3,2},{4,3},{5,4},{6,5},{7,6},{8,7},{9,8},{10,9},{11,1... | collective-permute-start | bytes 786440 | tf_op jit(solution)/shard_map/ppermute | solution.py:21
  221.9 11.0 %collective-permute-start.29 = (bf16[4,1,256,128]{3,2,0,1:T(8,128)(2,1)S(1)}, bf16[4,1,256,128]{3,2,0,1:T(8,128)(2,1)S(1)}, u32[]{:S(2)}, u32[]{:S(2)}) collective-permute-start(bf16[4,1,256,128]{3,2,0,1:T(8,128)(2,1)S(1)} %pad_maximum_fusion.10), channel_id=1, source_target_pairs={{0,1},{1,2},{2,3},{3,4},{4,5},{5,6},{6,7},{7,8},{8,9},{9,10},{10,1... | collective-permute-start | bytes 786440 | tf_op jit(solution)/shard_map/ppermute | solution.py:18
  234.7 6.9 %collective-permute-start.31 = (bf16[2,1,256,128]{3,2,0,1:T(8,128)(2,1)S(1)}, bf16[2,1,256,128]{3,2,0,1:T(8,128)(2,1)S(1)}, u32[]{:S(2)}, u32[]{:S(2)}) collective-permute-start(bf16[2,1,256,128]{3,2,0,1:T(8,128)(2,1)S(1)} %bitcast.340), channel_id=1, source_target_pairs={{128,0},{256,128},{384,256},{129,1},{257,129},{385,257},{130,2},{2... | collective-permute-start | bytes 393224 | tf_op jit(solution)/shard_map/ppermute | solution.py:10
  241.6 5.8 %collective-permute-start.33 = (bf16[4,1,256,128]{3,2,0,1:T(8,128)(2,1)S(1)}, bf16[4,1,256,128]{3,2,0,1:T(8,128)(2,1)S(1)}, u32[]{:S(2)}, u32[]{:S(2)}) collective-permute-start(bf16[4,1,256,128]{3,2,0,1:T(8,128)(2,1)S(1)} %pad_maximum_fusion.11), channel_id=1, source_target_pairs={{1,0},{2,1},{3,2},{4,3},{5,4},{6,5},{7,6},{8,7},{9,8},{10,9},{11,1... | collective-permute-start | bytes 786440 | tf_op jit(solution)/shard_map/ppermute | solution.py:21
  243.6 11.0 %collective-permute-start.32 = (bf16[4,1,256,128]{3,2,0,1:T(8,128)(2,1)S(1)}, bf16[4,1,256,128]{3,2,0,1:T(8,128)(2,1)S(1)}, u32[]{:S(2)}, u32[]{:S(2)}) collective-permute-start(bf16[4,1,256,128]{3,2,0,1:T(8,128)(2,1)S(1)} %pad_maximum_fusion.11), channel_id=1, source_target_pairs={{0,1},{1,2},{2,3},{3,4},{4,5},{5,6},{6,7},{7,8},{8,9},{9,10},{10,1... | collective-permute-start | bytes 786440 | tf_op jit(solution)/shard_map/ppermute | solution.py:18
  (157 other events, 2049.6 us)
where the time goes:
time: 260 us; the launch traced here: 257 us
  starting transfers between devices  103 us (40%)
  waiting for transfers between devices  79 us (30%)
  local copies, waits for them, and re-layouts  39.5 us (15%)
  other arithmetic  16.7 us (6%)
  matrix products  15.7 us (6%)
  between operations  3.03 us (1%)
    ppermute x12, waiting for transfers between devices, extended_2(): lax.ppermute(lax.slice_in_dim(block, block.shape[dim] - width, None, axis...  43.5 us
    ppermute x12, starting transfers between devices, extended_2(): lax.ppermute(lax.slice_in_dim(block, 0, width, axis=dim), axis, backward)  34.2 us
    ppermute x12, starting transfers between devices, extended_2(): lax.ppermute(lax.slice_in_dim(block, block.shape[dim] - width, None, axis...  33.4 us
    ppermute x10, starting transfers between devices, from_behind(): return lax.ppermute(block, axis, route)  24.3 us
    ppermute x10, waiting for transfers between devices, from_behind(): return lax.ppermute(block, axis, route)  23.3 us
    concatenate x2, local copies, waits for them, and re-layouts, dense_conv(): jnp.concatenate(tap_list, axis=-1)  20.1 us
    all_to_all x1, starting transfers between devices, on_device(): lax.all_to_all(target, 'wa', split_axis=1, concat_axis=2, tiled=True)  10.8 us
    slice x6, local copies, waits for them, and re-layouts, dense_conv(): extended[step_t:step_t + frame_count, step_h:step_h + row_count, step_w:s...  8.41 us
  transfers between devices with their start and end apart: 35, of which 19 were waited for; matrix products, arithmetic and copies ran while one was open for 21% of the time, Pallas kernels for 0%

commit v1 on v0

v1 whole, which is shorter than its diff:
```python
import jax
import jax.numpy as jnp
from jax import lax
from jax.experimental import pallas as pl
from jax.experimental.pallas import tpu as pltpu
from jax.sharding import PartitionSpec as P

MESH = pl.DeviceIdType.MESH
F32, BF16 = jnp.float32, jnp.bfloat16
SIDES = [(0, -1), (0, 1), (-1, 0), (1, 0), (-1, -1), (-1, 1), (1, -1), (1, 1)]
CT, CS, WIDE = 192, 128, 256
NTA, NHA, NWA = 4, 4, 32
GRID_R, GRID_C = NTA * NHA, NWA
TRANSPOSED = (((1,), (1,)), ((), ()))


def rational(x):
    gate = 0.5 * jnp.tanh(0.5 * x) + 0.5
    return x * gate


def act(s):
    gate = 0.5 * jnp.tanh(0.5 * s) + 0.5
    u = s * gate
    return u, gate + u * (1.0 - gate)


def silu_norm(x):
    scale = lax.rsqrt(jnp.sum(x * x, axis=-1, keepdims=True) * (1.0 / CT) + 1e-06)
    return rational(x * scale)


def shifted(v, by, frames):
    if by > 0:
        return jnp.where(frames >= by, pltpu.roll(v, by, v.ndim - 2), 0.0)
    return jnp.where(frames < 8 + by, pltpu.roll(v, 8 + by, v.ndim - 2), 0.0)


def kernel(
    tin, tw, sin, dw, pw, proj, out,
    xin, xf, xt, hact, hsec, af, lhs, wb, pp,
    rin, rf, s0f, s2f, u12, u10, mm10, mm8, sl0, sl1, sl2, sl3, d10, d8,
    h0, h2, h4, h6, gf, s4b, mb, pr, ob, dwv, pwv, projv,
    wsem, xsend, xrecv, rsend, rrecv, osend, orecv, hsend, hrecv,
):
    ta, ha, wa = lax.axis_index("ta"), lax.axis_index("ha"), lax.axis_index("wa")
    row, col = ha * NTA + ta, wa
    band, line = lax.div(wa, 8), lax.rem(wa, 8)
    has_self = band == ta

    def at(a, b, c):
        return {"ta": a, "ha": b, "wa": c}

    def near(dr, dc):
        r = row + dr
        return at(lax.rem(r + GRID_R, NTA), lax.div(r + GRID_R, NTA) - NHA, col + dc)

    def there(dr, dc):
        r, c = row + dr, col + dc
        return (r >= 0) & (r < GRID_R) & (c >= 0) & (c < GRID_C)

    weights = []
    for b in range(2):
        for i in range(3):
            weights.append(
                pltpu.make_async_copy(
                    tw.at[0, b, i], wb.at[b, i, :, :, 0:CT, :], wsem.at[b * 3 + i]
                )
            )
    small = [
        pltpu.make_async_copy(dw, dwv, wsem.at[6]),
        pltpu.make_async_copy(pw, pwv, wsem.at[7]),
        pltpu.make_async_copy(proj, projv, wsem.at[8]),
    ]
    for copy in small + weights:
        copy.start()

    for buf in (hact, hsec, h0, h2, h4, h6, af):
        buf[...] = jnp.zeros_like(buf)
    wb[:, :, :, :, CT:WIDE, :] = jnp.zeros((2, 3, 3, 3, WIDE - CT, CT), BF16)

    barrier = pltpu.get_barrier_semaphore()

    def greet(device):
        pl.semaphore_signal(barrier, inc=1, device_id=device, device_id_type=MESH)

    @pl.loop(0, NWA)
    def _(c):
        @pl.when(jnp.logical_not(has_self & (c == wa)))
        def _():
            greet(at(band, ha, c))

    @pl.loop(0, 32)
    def _(m):
        x, y = lax.div(m, 8), ta * 8 + lax.rem(m, 8)

        @pl.when(jnp.logical_not((x == ta) & (y == wa)))
        def _():
            greet(at(x, ha, y))

    for dx in range(1, NTA):
        greet(at(lax.rem(ta + dx, NTA), ha, wa))
    near_count = 0
    for dr, dc in SIDES:
        present = there(dr, dc)
        near_count = near_count + present.astype(jnp.int32)

        @pl.when(present)
        def _():
            greet(near(dr, dc))

    pl.semaphore_wait(barrier, 64 - 2 * has_self.astype(jnp.int32) + 3 + near_count)

    def slab_copy(dx):
        x = lax.rem(ta + dx, NTA)
        return pltpu.make_async_remote_copy(
            src_ref=tin.at[:, pl.ds(x * 8, 8)],
            dst_ref=xin.at[pl.ds(ta * 2, 2)],
            send_sem=xsend.at[dx],
            recv_sem=xrecv.at[dx],
            device_id=at(x, ha, wa),
            device_id_type=MESH,
        )

    own_slab = pltpu.make_async_copy(
        tin.at[:, pl.ds(ta * 8, 8)], xin.at[pl.ds(ta * 2, 2)], xrecv.at[0]
    )
    for dx in range(1, NTA):
        slab_copy(dx).start()
    own_slab.start()

    @pl.loop(0, NWA)
    def _(step):
        c = lax.rem(wa + step, NWA)
        itself = has_self & (step == 0)

        @pl.when(itself)
        def _():
            pltpu.make_async_copy(sin.at[:, c], rin.at[pl.ds(ta * 2, 2), line], rrecv).start()

        @pl.when(jnp.logical_not(itself))
        def _():
            pltpu.make_async_remote_copy(
                src_ref=sin.at[:, c],
                dst_ref=rin.at[pl.ds(ta * 2, 2), line],
                send_sem=rsend,
                recv_sem=rrecv,
                device_id=at(band, ha, c),
                device_id_type=MESH,
            ).start()

    def side_copy(buf, k, slot, d):
        dr, dc = SIDES[d]
        source = {-1: (k, k), 0: (k, 8), 1: (8, k)}
        target = {-1: (8 + k, k), 0: (k, 8), 1: (0, k)}
        rs, cs, rt, ct = source[dr], source[dc], target[dr], target[dc]
        return pltpu.make_async_remote_copy(
            src_ref=buf.at[pl.ds(*rs), pl.ds(*cs)],
            dst_ref=buf.at[pl.ds(*rt), pl.ds(*ct)],
            send_sem=hsend.at[slot, d],
            recv_sem=hrecv.at[slot, d],
            device_id=near(dr, dc),
            device_id_type=MESH,
        )

    def send(buf, k, slot):
        for d, (dr, dc) in enumerate(SIDES):
            @pl.when(there(dr, dc))
            def _():
                side_copy(buf, k, slot, d).start()

    def receive(buf, k, slot):
        for d, (dr, dc) in enumerate(SIDES):
            @pl.when(there(-dr, -dc))
            def _():
                side_copy(buf, k, slot, d).wait_recv()

    def drain(buf, k, slot):
        for d, (dr, dc) in enumerate(SIDES):
            @pl.when(there(dr, dc))
            def _():
                side_copy(buf, k, slot, d).wait_send()

    def ring(k):
        full = 8 + 2 * k
        return [
            (slice(0, k), slice(0, full)),
            (slice(8 + k, full), slice(0, full)),
            (slice(k, 8 + k), slice(0, k)),
            (slice(k, 8 + k), slice(8 + k, full)),
        ]

    def clear_outside(buf):
        @pl.when(row == 0)
        def _():
            buf[0] = jnp.zeros_like(buf[0])

        @pl.when(row == GRID_R - 1)
        def _():
            buf[9] = jnp.zeros_like(buf[9])

        @pl.when(col == 0)
        def _():
            buf[:, 0] = jnp.zeros_like(buf[:, 0])

        @pl.when(col == GRID_C - 1)
        def _():
            buf[:, 9] = jnp.zeros_like(buf[:, 9])

    frames = lax.broadcasted_iota(jnp.int32, (1, 8, CS), 1)
    wide_frames = lax.broadcasted_iota(jnp.int32, (1, 8, CT), 1)

    def taps(src, h, width, n, flip):
        acc = [None] * 3
        for j in range(3):
            for l in range(3):
                x = src[h + j, l : l + width]
                for i in range(3):
                    jj, ll = (2 - j, 2 - l) if flip else (j, l)
                    term = x * dwv[n, i, jj, ll : ll + 1, :].reshape(1, 1, CS)
                    acc[i] = term if acc[i] is None else acc[i] + term
        sign = -1 if flip else 1
        return acc[2] + shifted(acc[1], sign, frames) + shifted(acc[0], 2 * sign, frames)

    def conv(b):
        for j in range(3):
            for l in range(3):
                at_lane = (j * 3 + l) * WIDE
                lhs[:, at_lane : at_lane + WIDE] = (
                    af[j : j + 8, l : l + 8].reshape(512, WIDE).astype(BF16)
                )
        for i in range(3):
            weights[b * 3 + i].wait()
            pp[i] = jnp.dot(
                lhs[...], wb[b, i].reshape(9 * WIDE, CT), preferred_element_type=F32
            )

    def conv_row(h):
        p = [pp[i, pl.ds(h * 64, 64)].reshape(8, 8, CT) for i in range(3)]
        return p[2] + shifted(p[1], 1, wide_frames) + shifted(p[0], 2, wide_frames)

    own_slab.wait()
    for dx in range(1, NTA):
        slab_copy(dx).wait_recv()
    xall = xin[...].astype(F32).reshape(512, CT)
    xf[0] = xall[:, 0:CS]
    xf[1, :, 0 : CT - CS] = xall[:, CS:CT]

    @pl.loop(0, 8)
    def _(h):
        for w in range(8):
            place = pl.ds(h * 8 + w, 8, stride=64)
            x = jnp.concatenate([xf[0, place, :], xf[1, place, :][:, 0 : CT - CS]], axis=-1)
            xt[h, w] = x
            a = silu_norm(x)
            hact[h + 1, w + 1] = a.astype(BF16)
            af[h + 1, w + 1, :, 0:CT] = a

    send(hact, 1, 0)

    pltpu.make_async_copy(rin, rin, rrecv).wait()
    rf[...] = rin[...].astype(F32).reshape(512, CS)

    @pl.loop(0, 8)
    def _(h):
        for w in range(8):
            s = rf[pl.ds(h * 8 + w, 8, stride=64), :]
            s0f[h + 2, w + 2] = s
            h0[h + 2, w + 2] = s.astype(BF16)
            u, slope = act(s)
            u12[h + 2, w + 2] = u
            sl0[h, w] = slope

    send(h0, 2, 1)

    receive(hact, 1, 0)
    for rows, cols in ring(1):
        af[rows, cols, :, 0:CT] = hact[rows, cols].astype(F32)
    conv(0)

    @pl.loop(0, 8)
    def _(h):
        a = silu_norm(conv_row(h))
        hsec[h + 1, 1:9] = a.astype(BF16)
        af[h + 1, 1:9, :, 0:CT] = a

    send(hsec, 1, 2)

    for copy in small:
        copy.wait()

    def border(buf, field):
        for rows, cols in ring(2):
            s = buf[rows, cols].astype(F32)
            field[rows, cols] = s
            u12[rows, cols] = act(s)[0]

    def wide_layer(n, field, slope_buf):
        @pl.loop(0, 10)
        def _(h):
            d10[h] = taps(u12, h, 10, n, False).reshape(80, CS).astype(BF16)

        mm10[...] = jnp.dot(
            d10[...].reshape(800, CS), pwv[n], preferred_element_type=F32
        ).reshape(10, 10, 8, CS)

        @pl.loop(0, 10)
        def _(h):
            s = field[h + 1, 1:11] + mm10[h]
            mm10[h] = s
            u, slope = act(s)
            u10[h] = u
            slope_buf[h] = slope

        clear_outside(u10)

    def narrow_layer(n):
        @pl.loop(0, 8)
        def _(h):
            d8[h] = taps(u10, h, 8, n, False).reshape(64, CS).astype(BF16)

        mm8[...] = jnp.dot(
            d8[...].reshape(512, CS), pwv[n], preferred_element_type=F32
        ).reshape(8, 8, 8, CS)

    receive(h0, 2, 1)
    border(h0, s0f)
    wide_layer(0, s0f, sl1)
    narrow_layer(1)

    @pl.loop(0, 8)
    def _(h):
        s = mm10[h + 1, 1:9] + mm8[h]
        s2f[h + 2, 2:10] = s
        h2[h + 2, 2:10] = s.astype(BF16)
        u, slope = act(s)
        u12[h + 2, 2:10] = u
        sl2[h] = slope

    send(h2, 2, 3)

    receive(hsec, 1, 2)
    for rows, cols in ring(1):
        af[rows, cols, :, 0:CT] = hsec[rows, cols].astype(F32)
    conv(1)

    receive(h2, 2, 3)
    border(h2, s2f)
    wide_layer(2, s2f, sl3)
    narrow_layer(3)

    @pl.loop(0, 8)
    def _(h):
        s4b[h] = (mm10[h + 1, 1:9] + mm8[h]).reshape(64, CS).astype(BF16)

    pr[...] = jnp.dot(
        s4b[...].reshape(512, CS), projv[...], preferred_element_type=F32
    ).reshape(8, 64, CT)

    @pl.loop(0, 8)
    def _(h):
        target = (xt[h] + conv_row(h)).reshape(64, CT)
        mb[h] = (pr[h] - target).astype(BF16)

    mm8[...] = lax.dot_general(
        mb[...].reshape(512, CT), projv[...], TRANSPOSED, preferred_element_type=F32
    ).reshape(8, 8, 8, CS)

    @pl.loop(0, 8)
    def _(h):
        g = mm8[h]
        gf[h + 2, 2:10] = g
        h4[h + 2, 2:10] = g.astype(BF16)

    send(h4, 2, 4)

    def wide_back(n, buf, slot, slope_buf):
        receive(buf, 2, slot)
        for rows, cols in ring(2):
            gf[rows, cols] = buf[rows, cols].astype(F32)
        u12[...] = lax.dot_general(
            gf[...].reshape(1152, CS).astype(BF16), pwv[n], TRANSPOSED, preferred_element_type=F32
        ).reshape(12, 12, 8, CS)

        @pl.loop(0, 10)
        def _(h):
            mm10[h] = gf[h + 1, 1:11] + taps(u12, h, 10, n, True) * slope_buf[h]

        clear_outside(mm10)
        u10[...] = lax.dot_general(
            mm10[...].reshape(800, CS).astype(BF16),
            pwv[n - 1],
            TRANSPOSED,
            preferred_element_type=F32,
        ).reshape(10, 10, 8, CS)

    wide_back(3, h4, 4, sl3)

    @pl.loop(0, 8)
    def _(h):
        g = mm10[h + 1, 1:9] + taps(u10, h, 8, 2, True) * sl2[h]
        gf[h + 2, 2:10] = g
        h6[h + 2, 2:10] = g.astype(BF16)

    send(h6, 2, 5)
    wide_back(1, h6, 5, sl1)

    @pl.loop(0, 8)
    def _(h):
        g = mm10[h + 1, 1:9] + taps(u10, h, 8, 0, True) * sl0[h]
        rf[pl.ds(h * 64, 64)] = g.reshape(64, CS)

    @pl.loop(0, 8)
    def _(h):
        for t in range(8):
            ob[t, h] = rf[pl.ds(h * 64 + t, 8, stride=8), :].astype(BF16)

    @pl.loop(0, 32)
    def _(m):
        spot = lax.rem(m + wa, 32)
        x, h = lax.div(spot, 8), lax.rem(spot, 8)
        itself = (x == ta) & (ta * 8 + h == wa)

        @pl.when(itself)
        def _():
            pltpu.make_async_copy(ob.at[pl.ds(x * 2, 2), h], out.at[:, wa], orecv).start()

        @pl.when(jnp.logical_not(itself))
        def _():
            pltpu.make_async_remote_copy(
                src_ref=ob.at[pl.ds(x * 2, 2), h],
                dst_ref=out.at[:, wa],
                send_sem=osend,
                recv_sem=orecv,
                device_id=at(x, ha, ta * 8 + h),
                device_id_type=MESH,
            ).start()

    for buf, k, slot in (
        (hact, 1, 0), (h0, 2, 1), (hsec, 1, 2), (h2, 2, 3), (h4, 2, 4), (h6, 2, 5)
    ):
        drain(buf, k, slot)
    for dx in range(1, NTA):
        slab_copy(dx).wait_send()
    pltpu.make_async_copy(out, out, orecv).wait()

    for sem in (rsend, osend):
        @pl.when(has_self)
        def _():
            part = sin.at[:, 0:31]
            pltpu.make_async_copy(part, part, sem).wait()

        @pl.when(jnp.logical_not(has_self))
        def _():
            pltpu.make_async_copy(sin, sin, sem).wait()


def on_device(tin, tw, sin, dw, pw, proj):
    anywhere = pl.BlockSpec(memory_space=pl.ANY)
    tile = lambda rows, cols, c, kind: pltpu.VMEM((rows, cols, 8, c), kind)
    dma = pltpu.SemaphoreType.DMA
    scratch = [
        pltpu.VMEM((8, 8, 8, CT), BF16),
        pltpu.VMEM((2, 512, CS), F32),
        tile(8, 8, CT, F32),
        tile(10, 10, CT, BF16),
        tile(10, 10, CT, BF16),
        tile(10, 10, WIDE, F32),
        pltpu.VMEM((512, 9 * WIDE), BF16),
        pltpu.VMEM((2, 3, 3, 3, WIDE, CT), BF16),
        pltpu.VMEM((3, 512, CT), F32),
        pltpu.VMEM((8, 8, 8, CS), BF16),
        pltpu.VMEM((512, CS), F32),
        tile(12, 12, CS, F32),
        tile(12, 12, CS, F32),
        tile(12, 12, CS, F32),
        tile(10, 10, CS, F32),
        tile(10, 10, CS, F32),
        tile(8, 8, CS, F32),
        tile(8, 8, CS, F32),
        tile(10, 10, CS, F32),
        tile(8, 8, CS, F32),
        tile(10, 10, CS, F32),
        pltpu.VMEM((10, 80, CS), BF16),
        pltpu.VMEM((8, 64, CS), BF16),
        tile(12, 12, CS, BF16),
        tile(12, 12, CS, BF16),
        tile(12, 12, CS, BF16),
        tile(12, 12, CS, BF16),
        tile(12, 12, CS, F32),
        pltpu.VMEM((8, 64, CS), BF16),
        pltpu.VMEM((8, 64, CT), BF16),
        pltpu.VMEM((8, 64, CT), F32),
        pltpu.VMEM((8, 8, 8, CS), BF16),
        pltpu.VMEM((4, 3, 3, 3, CS), F32),
        pltpu.VMEM((4, CS, CS), BF16),
        pltpu.VMEM((CS, CT), BF16),
        dma((9,)),
        dma((NTA,)),
        dma((NTA,)),
        dma(()),
        dma(()),
        dma(()),
        dma(()),
        dma((6, 8)),
        dma((6, 8)),
    ]
    result = pl.pallas_call(
        kernel,
        out_shape=jax.ShapeDtypeStruct((2, 32, 8, CS), BF16),
        in_specs=[anywhere] * 6,
        out_specs=anywhere,
        scratch_shapes=scratch,
        compiler_params=pltpu.CompilerParams(
            collective_id=0, has_side_effects=True, vmem_limit_bytes=56 * 1024 * 1024
        ),
    )(tin, tw, sin.reshape(2, 32, 8, CS), dw, pw, proj)
    return result.reshape(2, 1, 256, CS)


def solution(mesh):
    rows = P("ta", ("ha", "wa"), None, None)
    return jax.shard_map(
        on_device,
        mesh=mesh,
        in_specs=(P("ta", "ha", "wa", None), P(), rows, P(), P(), P()),
        out_specs=rows,
        check_vma=False,
    )
```

time: 260 us -> 82 us (0.32)
  the two profiles are of different devices: /device:TPU:32 before, /device:TPU:41 now
where the time goes in v1:
time: 82 us; the launch traced here: 81.7 us
  Pallas kernels  77.1 us (94%)
  local copies, waits for them, and re-layouts  4.55 us (6%)
    pallas_call x1, Pallas kernels, on_device(): pl.pallas_call(kernel, out_shape=jax.ShapeDtypeStruct((2, 32, 8, CS), BF1...  77.1 us
    unnamed x3, local copies, waits for them, and re-layouts  4.55 us

profile of v1, /device:TPU:41, one launch (start us, length us, event | category | flops | bytes accessed | tf_op | source)
XLA Modules:
  0.0 81.7 jit_solution(8557813008629634837)
XLA Ops:
  0.0 1.5 %copy.8.proj = bf16[128,192]{1,0:T(8,128)(2,1)} copy(bf16[128,192]{0,1:T(8,128)(2,1)} %param.11) | data formatting | bytes 98304 | tf_op args[5]
  1.5 1.5 %copy.7.dw = f32[4,3,3,3,128]{4,3,2,1,0:T(4,128)} copy(f32[4,3,3,3,128]{4,0,3,2,1:T(4,128)} %param.9) | data formatting | bytes 110592 | tf_op args[3]
  3.0 77.1 %shard_map.64 = bf16[2,32,8,128]{3,2,1,0:T(8,128)(2,1)} custom-call(bf16[2,32,8,192]{3,2,1,0:T(8,128)(2,1)} %tin.1, bf16[1,2,3,3,3,192,192]{6,5,4,3,2,1,0:T(8,128)(2,1)} %tw.1, bf16[2,32,8,128]{3,2,1,0:T(8,128)(2,1)} %bitcast.5, f32[4,3,3,3,128]{4,3,2,1,0:T(4,128)} %copy.7.dw, bf16[4,128,128]{2,1,0:T(8,128)(2,1)} %pw.1, bf16[128,192]{1,0:T(8,128)(2,1)} %copy.8.proj), custom_call_target="tpu_custom_call" | custom-call | tf_op jit(solution)/shard_map/pallas_call | solution.py:508
  80.1 1.6 %copy.11 = bf16[2,1,256,128]{3,2,1,0:T(8,128)(2,1)} copy(bf16[2,1,256,128]{3,2,1,0:T(8,128)(2,1)} %bitcast.4) | data formatting | bytes 262144

commit v2 on v1

v2 whole, which is shorter than its diff:
```python
import jax
import jax.numpy as jnp
from jax import lax
from jax.experimental import pallas as pl
from jax.experimental.pallas import tpu as pltpu
from jax.sharding import PartitionSpec as P

MESH = pl.DeviceIdType.MESH
F32, BF16 = jnp.float32, jnp.bfloat16
SIDES = [(0, -1), (0, 1), (-1, 0), (1, 0), (-1, -1), (-1, 1), (1, -1), (1, 1)]
CT, CS, WIDE = 192, 128, 256
TH, TW = 4, 16
GRID_R, GRID_C = 32, 16
TRANSPOSED = (((1,), (1,)), ((), ()))


def rational(x):
    gate = 0.5 * jnp.tanh(0.5 * x) + 0.5
    return x * gate


def act(s):
    gate = 0.5 * jnp.tanh(0.5 * s) + 0.5
    u = s * gate
    return u, gate + u * (1.0 - gate)


def silu_norm(x):
    scale = lax.rsqrt(jnp.sum(x * x, axis=-1, keepdims=True) * (1.0 / CT) + 1e-06)
    return rational(x * scale)


def shifted(v, by, frames):
    if by > 0:
        return jnp.where(frames >= by, pltpu.roll(v, by, v.ndim - 2), 0.0)
    return jnp.where(frames < 8 + by, pltpu.roll(v, 8 + by, v.ndim - 2), 0.0)


def kernel(
    tin, tw, sin, dw, pw, proj, out,
    xin, xf, xt, hact, hsec, af, lhs, wb, pp,
    rin, rf, s0f, s2f, u20, u18, d18, mm18, d16, mm16, sl0, sl1, sl2,
    h0, h2, hs, hg, gf, eb, g22, g20, s4b, mb, pr, ob, dwv, pwv, projv,
    wsem, xsend, xrecv, rsend, rrecv, osend, orecv, hsend, hrecv,
):
    ta, ha, wa = lax.axis_index("ta"), lax.axis_index("ha"), lax.axis_index("wa")
    z, low = lax.div(wa, 4), lax.rem(wa, 4)

    def bent(p):
        return jnp.where(p < 2, p, 5 - p)

    def place(a, b):
        p = bent(b)
        return a * 4 + jnp.where(lax.rem(a, 2) == 0, p, 3 - p)

    row, col = ha * 8 + z, place(ta, low)

    def at(a, b, c):
        return {"ta": a, "ha": b, "wa": c}

    def owner(r, c):
        a, p = lax.div(c, 4), lax.rem(c, 4)
        p = bent(jnp.where(lax.rem(a, 2) == 0, p, 3 - p))
        return at(a, lax.div(r, 8), lax.rem(r, 8) * 4 + p)

    def near(dr, dc):
        return owner(row + dr, col + dc)

    def there(dr, dc):
        r, c = row + dr, col + dc
        return (r >= 0) & (r < GRID_R) & (c >= 0) & (c < GRID_C)

    weights = []
    for b in range(2):
        for i in range(3):
            weights.append(
                pltpu.make_async_copy(
                    tw.at[0, b, i], wb.at[b, i, :, :, 0:CT, :], wsem.at[b * 3 + i]
                )
            )
    small = [
        pltpu.make_async_copy(dw, dwv, wsem.at[6]),
        pltpu.make_async_copy(pw, pwv, wsem.at[7]),
        pltpu.make_async_copy(proj, projv, wsem.at[8]),
    ]
    for copy in small + weights:
        copy.start()

    def clear_outside(buf, k):
        @pl.when(row == 0)
        def _():
            buf[0:k] = jnp.zeros_like(buf[0:k])

        @pl.when(row == GRID_R - 1)
        def _():
            buf[TH + k :] = jnp.zeros_like(buf[TH + k :])

        @pl.when(col == 0)
        def _():
            buf[:, 0:k] = jnp.zeros_like(buf[:, 0:k])

        @pl.when(col == GRID_C - 1)
        def _():
            buf[:, TW + k :] = jnp.zeros_like(buf[:, TW + k :])

    halos = ((hact, 1, 0), (h0, 2, 1), (hsec, 1, 2), (h2, 2, 3), (hs, 3, 4), (hg, 4, 5))
    for buf, k, _ in halos:
        clear_outside(buf, k)

    barrier = pltpu.get_barrier_semaphore()

    def greet(device):
        pl.semaphore_signal(barrier, inc=1, device_id=device, device_id_type=MESH)

    spread_count = jnp.where(lax.div(wa, 2) == col, 7, 8)
    for step in range(8):
        r = ha * 8 + lax.rem(z + step, 8)

        @pl.when(jnp.logical_not((r == row) & (lax.div(wa, 2) == col)))
        def _():
            greet(owner(r, lax.div(wa, 2)))

    for step in range(8):
        a, b = step // 2, 2 * col + step % 2

        @pl.when(jnp.logical_not((a == ta) & (b == wa)))
        def _():
            greet(at(a, ha, b))

    gather_count = jnp.where(lax.div(wa, 2) == col, 7, 8)
    for step in range(1, 16):
        greet(owner(row, lax.rem(col + step, 16)))
    near_count = 0
    for dr, dc in SIDES:
        present = there(dr, dc)
        near_count = near_count + present.astype(jnp.int32)

        @pl.when(present)
        def _():
            greet(near(dr, dc))

    af[:, :, :, CS:WIDE] = jnp.zeros((TH + 2, TW + 2, 8, WIDE - CS), F32)
    wb[:, :, :, :, CT:WIDE, :] = jnp.zeros((2, 3, 3, 3, WIDE - CT, CT), BF16)
    pl.semaphore_wait(barrier, 15 + spread_count + gather_count + near_count)

    own_patch = pltpu.make_async_copy(
        tin.at[:, pl.ds(z * TH, TH)], xin.at[pl.ds(ta * 2, 2), :, lax.rem(wa, 2)], xrecv
    )
    patch_self = lax.div(wa, 2) == col
    for step in range(8):
        to = lax.rem(z + step, 8)

        def send_patch():
            pltpu.make_async_remote_copy(
                src_ref=tin.at[:, pl.ds(to * TH, TH)],
                dst_ref=xin.at[pl.ds(ta * 2, 2), :, lax.rem(wa, 2)],
                send_sem=xsend,
                recv_sem=xrecv,
                device_id=owner(ha * 8 + to, lax.div(wa, 2)),
                device_id_type=MESH,
            ).start()

        if step:
            send_patch()
        else:
            pl.when(patch_self)(own_patch.start)
            pl.when(jnp.logical_not(patch_self))(send_patch)

    pltpu.make_async_copy(
        sin.at[:, pl.ds(col * 2, 2)], rin.at[pl.ds(ta * 2, 2), low], rrecv
    ).start()
    for step in range(1, 16):
        c = lax.rem(col + step, 16)
        pltpu.make_async_remote_copy(
            src_ref=sin.at[:, pl.ds(c * 2, 2)],
            dst_ref=rin.at[pl.ds(ta * 2, 2), low],
            send_sem=rsend,
            recv_sem=rrecv,
            device_id=owner(row, c),
            device_id_type=MESH,
        ).start()

    def side_copy(buf, k, slot, d):
        dr, dc = SIDES[d]

        def source(side, size):
            return pl.ds(*{-1: (k, k), 0: (k, size), 1: (size, k)}[side])

        def target(side, size):
            return pl.ds(*{-1: (size + k, k), 0: (k, size), 1: (0, k)}[side])

        return pltpu.make_async_remote_copy(
            src_ref=buf.at[source(dr, TH), source(dc, TW)],
            dst_ref=buf.at[target(dr, TH), target(dc, TW)],
            send_sem=hsend.at[slot, d],
            recv_sem=hrecv.at[slot, d],
            device_id=near(dr, dc),
            device_id_type=MESH,
        )

    def send(buf, k, slot):
        for d, (dr, dc) in enumerate(SIDES):
            @pl.when(there(dr, dc))
            def _():
                side_copy(buf, k, slot, d).start()

    def receive(buf, k, slot):
        for d, (dr, dc) in enumerate(SIDES):
            @pl.when(there(-dr, -dc))
            def _():
                side_copy(buf, k, slot, d).wait_recv()

    def drain(buf, k, slot):
        for d, (dr, dc) in enumerate(SIDES):
            @pl.when(there(dr, dc))
            def _():
                side_copy(buf, k, slot, d).wait_send()

    def ring(k):
        rows, cols = TH + 2 * k, TW + 2 * k
        return [
            (slice(0, k), slice(0, cols)),
            (slice(TH + k, rows), slice(0, cols)),
            (slice(k, TH + k), slice(0, k)),
            (slice(k, TH + k), slice(TW + k, cols)),
        ]

    frames = lax.broadcasted_iota(jnp.int32, (1, 8, CS), 1)
    wide_frames = lax.broadcasted_iota(jnp.int32, (1, 8, CT), 1)

    def taps(src, h, start, width, n, flip):
        acc = [None] * 3
        for j in range(3):
            for l in range(3):
                x = src[h + j, start + l : start + l + width]
                for i in range(3):
                    jj, ll = (2 - j, 2 - l) if flip else (j, l)
                    term = x * dwv[i, jj, ll, n : n + 1, :].reshape(1, 1, CS)
                    acc[i] = term if acc[i] is None else acc[i] + term
        sign = -1 if flip else 1
        return acc[2] + shifted(acc[1], sign, frames) + shifted(acc[0], 2 * sign, frames)

    def conv(b):
        for j in range(3):
            for l in range(3):
                at_lane = (j * 3 + l) * WIDE
                lhs[:, at_lane : at_lane + WIDE] = (
                    af[j : j + TH, l : l + TW].reshape(512, WIDE).astype(BF16)
                )
        for i in range(3):
            weights[b * 3 + i].wait()
            pp[i] = jnp.dot(
                lhs[...], wb[b, i].reshape(9 * WIDE, CT), preferred_element_type=F32
            )

    def conv_row(m):
        p = [pp[i, pl.ds(m * 64, 64)].reshape(8, 8, CT) for i in range(3)]
        return p[2] + shifted(p[1], 1, wide_frames) + shifted(p[0], 2, wide_frames)

    pltpu.make_async_copy(rin, rin, rrecv).wait()
    rf[...] = rin[...].astype(F32).reshape(512, CS)

    @pl.loop(0, TH)
    def _(h):
        for w in range(TW):
            s = rf[pl.ds(h * TW + w, 8, stride=64), :]
            s0f[h + 2, w + 2] = s
            h0[h + 2, w + 2] = s.astype(BF16)
            u, slope = act(s)
            u20[h + 2, w + 2] = u
            sl0[h, w] = slope

    send(h0, 2, 1)

    pltpu.make_async_copy(xin, xin, xrecv).wait()
    xall = xin[...].astype(F32).reshape(512, CT)
    xf[0] = xall[:, 0:CS]
    xf[1, :, 0 : CT - CS] = xall[:, CS:CT]

    @pl.loop(0, TH)
    def _(h):
        for w in range(TW):
            spot = pl.ds(h * TW + w, 8, stride=64)
            x = jnp.concatenate([xf[0, spot, :], xf[1, spot, :][:, 0 : CT - CS]], axis=-1)
            xt[h, w] = x
            a = silu_norm(x)
            hact[h + 1, w + 1] = a.astype(BF16)
            af[h + 1, w + 1, :, 0:CT] = a

    send(hact, 1, 0)

    for copy in small:
        copy.wait()

    def wide_layer(n, field):
        @pl.loop(0, TH + 2)
        def _(h):
            for w in (0, 9):
                d18[h, w : w + 9] = taps(u20, h, w, 9, n, False)

        mm18[...] = jnp.dot(
            d18[...].reshape(864, CS).astype(BF16), pwv[n], preferred_element_type=F32
        ).reshape(6, 18, 8, CS)

        @pl.loop(0, TH + 2)
        def _(h):
            s = field[h + 1, 1:19] + mm18[h]
            mm18[h] = s
            u, slope = act(s)
            u18[h] = u
            sl1[h] = slope

        clear_outside(u18, 1)

    def narrow_layer(n):
        @pl.loop(0, TH)
        def _(h):
            for w in (0, 8):
                d16[h, w : w + 8] = taps(u18, h, w, 8, n, False)

        mm16[...] = jnp.dot(
            d16[...].reshape(512, CS).astype(BF16), pwv[n], preferred_element_type=F32
        ).reshape(4, 16, 8, CS)

    receive(h0, 2, 1)
    for rows, cols in ring(2):
        s = h0[rows, cols].astype(F32)
        s0f[rows, cols] = s
        u20[rows, cols] = act(s)[0]
    wide_layer(0, s0f)
    narrow_layer(1)

    @pl.loop(0, TH)
    def _(h):
        s = mm18[h + 1, 1:17] + mm16[h]
        s2f[h + 2, 2:18] = s
        h2[h + 2, 2:18] = s.astype(BF16)
        u, slope = act(s)
        u20[h + 2, 2:18] = u
        sl2[h + 2, 2:18] = slope

    send(h2, 2, 3)

    receive(hact, 1, 0)
    for rows, cols in ring(1):
        af[rows, cols, :, 0:CT] = hact[rows, cols].astype(F32)
    conv(0)

    @pl.loop(0, 8)
    def _(m):
        h, w = lax.div(m, 2), lax.rem(m, 2) * 8
        a = silu_norm(conv_row(m))
        hsec[h + 1, pl.ds(w + 1, 8)] = a.astype(BF16)
        af[h + 1, pl.ds(w + 1, 8), :, 0:CT] = a

    send(hsec, 1, 2)

    receive(h2, 2, 3)
    for rows, cols in ring(2):
        s = h2[rows, cols].astype(F32)
        s2f[rows, cols] = s
        u, slope = act(s)
        u20[rows, cols] = u
        sl2[rows, cols] = slope

    @pl.loop(0, TH + 2)
    def _(h):
        for w in (0, 9):
            d18[h, w : w + 9] = taps(u20, h, w, 9, 2, False)

    mm18[...] = jnp.dot(
        d18[...].reshape(864, CS).astype(BF16), pwv[2], preferred_element_type=F32
    ).reshape(6, 18, 8, CS)

    @pl.loop(0, TH + 2)
    def _(h):
        s = s2f[h + 1, 1:19] + mm18[h]
        mm18[h] = s
        u, slope = act(s)
        u18[h] = u
        d18[h] = slope

    hs[3:7, 3:19] = d18[1:5, 1:17].astype(BF16)
    send(hs, 3, 4)
    clear_outside(u18, 1)
    narrow_layer(3)
    s4b[...] = (mm18[1:5, 1:17] + mm16[...]).reshape(512, CS).astype(BF16)

    pr[...] = lax.dot_general(s4b[...], projv[...], TRANSPOSED, preferred_element_type=F32)

    receive(hsec, 1, 2)
    for rows, cols in ring(1):
        af[rows, cols, :, 0:CT] = hsec[rows, cols].astype(F32)
    conv(1)

    @pl.loop(0, 8)
    def _(m):
        h, w = lax.div(m, 2), lax.rem(m, 2) * 8
        target = (xt[h, pl.ds(w, 8)] + conv_row(m)).reshape(64, CT)
        span = pl.ds(m * 64, 64)
        mb[span] = (pr[span] - target).astype(BF16)

    g = jnp.dot(mb[...], projv[...], preferred_element_type=F32).reshape(4, 16, 8, CS)
    gf[4:8, 4:20] = g
    hg[4:8, 4:20] = g.astype(BF16)
    send(hg, 4, 5)

    receive(hs, 3, 4)
    receive(hg, 4, 5)
    for rows, cols in ring(4):
        gf[rows, cols] = hg[rows, cols].astype(F32)

    def back(n, source, k):
        rows, cols = TH + 2 * k, TW + 2 * k
        eb[0:rows, 0:cols] = lax.dot_general(
            source[...].reshape(rows * cols * 8, CS).astype(BF16),
            pwv[n],
            TRANSPOSED,
            preferred_element_type=F32,
        ).reshape(rows, cols, 8, CS)

    back(3, gf, 4)

    @pl.loop(0, 10)
    def _(h):
        for w in (0, 11):
            slope = hs[h, w : w + 11].astype(F32)
            g22[h, w : w + 11] = (
                gf[h + 1, w + 1 : w + 12] + taps(eb, h, w, 11, 3, True) * slope
            )

    clear_outside(g22, 3)
    back(2, g22, 3)

    @pl.loop(0, 8)
    def _(h):
        for w in (0, 10):
            g20[h, w : w + 10] = (
                g22[h + 1, w + 1 : w + 11]
                + taps(eb, h, w, 10, 2, True) * sl2[h, w : w + 10]
            )

    clear_outside(g20, 2)
    back(1, g20, 2)

    @pl.loop(0, 6)
    def _(h):
        for w in (0, 9):
            d18[h, w : w + 9] = (
                g20[h + 1, w + 1 : w + 10]
                + taps(eb, h, w, 9, 1, True) * sl1[h, w : w + 9]
            )

    clear_outside(d18, 1)
    back(0, d18, 1)

    @pl.loop(0, 4)
    def _(h):
        for w in (0, 8):
            g = (
                d18[h + 1, w + 1 : w + 9]
                + taps(eb, h, w, 8, 0, True) * sl0[h, w : w + 8]
            )
            rf[pl.ds(h * 128 + w * 8, 64)] = g.reshape(64, CS)

    @pl.loop(0, TH)
    def _(h):
        for half in range(2):
            for t in range(8):
                ob[t, h, half] = rf[
                    pl.ds(h * 128 + half * 64 + t, 8, stride=8), :
                ].astype(BF16)

    for step in range(16):
        x, y = lax.rem(ta + step // 4, 4), lax.rem(low + step % 4, 4)
        source = ob.at[pl.ds(x * 2, 2), y]
        if step:
            pltpu.make_async_remote_copy(
                src_ref=source,
                dst_ref=out.at[:, pl.ds(col * 2, 2)],
                send_sem=osend,
                recv_sem=orecv,
                device_id=at(x, ha, z * 4 + y),
                device_id_type=MESH,
            ).start()
        else:
            pltpu.make_async_copy(source, out.at[:, pl.ds(col * 2, 2)], orecv).start()

    for buf, k, slot in halos:
        drain(buf, k, slot)

    @pl.when(patch_self)
    def _():
        part = tin.at[:, 0:28]
        pltpu.make_async_copy(part, part, xsend).wait()

    @pl.when(jnp.logical_not(patch_self))
    def _():
        pltpu.make_async_copy(tin, tin, xsend).wait()

    part = sin.at[:, 0:30]
    pltpu.make_async_copy(part, part, rsend).wait()
    pltpu.make_async_copy(part, part, osend).wait()
    pltpu.make_async_copy(out, out, orecv).wait()


def on_device(tin, tw, sin, dw, pw, proj):
    anywhere = pl.BlockSpec(memory_space=pl.ANY)
    dma = pltpu.SemaphoreType.DMA

    def tile(k, c, kind):
        return pltpu.VMEM((TH + 2 * k, TW + 2 * k, 8, c), kind)

    scratch = [
        pltpu.VMEM((8, TH, 2, 8, CT), BF16),
        pltpu.VMEM((2, 512, CS), F32),
        tile(0, CT, F32),
        tile(1, CT, BF16),
        tile(1, CT, BF16),
        tile(1, WIDE, F32),
        pltpu.VMEM((512, 9 * WIDE), BF16),
        pltpu.VMEM((2, 3, 3, 3, WIDE, CT), BF16),
        pltpu.VMEM((3, 512, CT), F32),
        pltpu.VMEM((8, TH, 2, 8, CS), BF16),
        pltpu.VMEM((512, CS), F32),
        tile(2, CS, F32),
        tile(2, CS, F32),
        tile(2, CS, F32),
        tile(1, CS, F32),
        tile(1, CS, F32),
        tile(1, CS, F32),
        tile(0, CS, F32),
        tile(0, CS, F32),
        tile(0, CS, F32),
        tile(1, CS, F32),
        tile(2, CS, F32),
        tile(2, CS, BF16),
        tile(2, CS, BF16),
        tile(3, CS, BF16),
        tile(4, CS, BF16),
        tile(4, CS, F32),
        tile(4, CS, F32),
        tile(3, CS, F32),
        tile(2, CS, F32),
        pltpu.VMEM((512, CS), BF16),
        pltpu.VMEM((512, CT), BF16),
        pltpu.VMEM((512, CT), F32),
        pltpu.VMEM((8, TH, 2, 8, CS), BF16),
        pltpu.VMEM((3, 3, 3, 4, CS), F32),
        pltpu.VMEM((4, CS, CS), BF16),
        pltpu.VMEM((CT, CS), BF16),
        dma((9,)),
        dma(()),
        dma(()),
        dma(()),
        dma(()),
        dma(()),
        dma(()),
        dma((6, 8)),
        dma((6, 8)),
    ]
    result = pl.pallas_call(
        kernel,
        out_shape=jax.ShapeDtypeStruct((2, 32, 8, CS), BF16),
        in_specs=[anywhere] * 6,
        out_specs=anywhere,
        scratch_shapes=scratch,
        compiler_params=pltpu.CompilerParams(
            collective_id=0, has_side_effects=True, vmem_limit_bytes=56 * 1024 * 1024
        ),
    )(tin, tw, sin.reshape(2, 32, 8, CS), dw.transpose(1, 2, 3, 0, 4), pw, proj.T)
    return result.reshape(2, 1, 256, CS)


def solution(mesh):
    rows = P("ta", ("ha", "wa"), None, None)
    return jax.shard_map(
        on_device,
        mesh=mesh,
        in_specs=(P("ta", "ha", "wa", None), P(), rows, P(), P(), P()),
        out_specs=rows,
        check_vma=False,
    )
```

time: 82 us -> 74.9 us (0.913)
  the two profiles are of different devices: /device:TPU:41 before, /device:TPU:57 now
where the time goes in v2:
time: 74.9 us; the launch traced here: 74.7 us
  Pallas kernels  73.2 us (98%)
  local copies, waits for them, and re-layouts  1.57 us (2%)
    pallas_call x1, Pallas kernels, on_device(): pl.pallas_call(kernel, out_shape=jax.ShapeDtypeStruct((2, 32, 8, CS), BF1...  73.2 us
    unnamed x1, local copies, waits for them, and re-layouts  1.57 us

profile of v2, /device:TPU:57, one launch (start us, length us, event | category | flops | bytes accessed | tf_op | source)
XLA Modules:
  0.0 74.7 jit_solution(7562073044361202914)
XLA Ops:
  0.0 73.2 %shard_map.64 = bf16[2,32,8,128]{3,2,1,0:T(8,128)(2,1)} custom-call(bf16[2,32,8,192]{3,2,1,0:T(8,128)(2,1)} %tin.1, bf16[1,2,3,3,3,192,192]{6,5,4,3,2,1,0:T(8,128)(2,1)} %tw.1, bf16[2,32,8,128]{3,2,1,0:T(8,128)(2,1)} %bitcast.7, f32[3,3,3,4,128]{4,3,2,1,0:T(4,128)} %bitcast.8, bf16[4,128,128]{2,1,0:T(8,128)(2,1)} %pw.1, bf16[192,128]{1,0:T(8,128)(2,1)} %bitcast.9), custom_call_target="tpu_custom_call" | custom-call | tf_op jit(solution)/shard_map/pallas_call | solution.py:562
  73.2 1.6 %copy.9 = bf16[2,1,256,128]{3,2,1,0:T(8,128)(2,1)} copy(bf16[2,1,256,128]{3,2,1,0:T(8,128)(2,1)} %bitcast.6) | data formatting | bytes 262144

commit v3 on v2

--- a/solution.py
+++ b/solution.py
@@ -7,10 +7,11 @@
 
 MESH = pl.DeviceIdType.MESH
 F32, BF16 = jnp.float32, jnp.bfloat16
-SIDES = [(0, -1), (0, 1), (-1, 0), (1, 0), (-1, -1), (-1, 1), (1, -1), (1, 1)]
+SIDES = [(-1, 0), (1, 0), (-1, -1), (-1, 1), (1, -1), (1, 1), (0, -1), (0, 1)]
+FAR_FIRST = (2, 1, 3, 0)
 CT, CS, WIDE = 192, 128, 256
-TH, TW = 4, 16
-GRID_R, GRID_C = 32, 16
+TH, TW = 8, 8
+GRID_R, GRID_C = 16, 32
 TRANSPOSED = (((1,), (1,)), ((), ()))
 
 
@@ -39,8 +40,8 @@
 def kernel(
     tin, tw, sin, dw, pw, proj, out,
     xin, xf, xt, hact, hsec, af, lhs, wb, pp,
-    rin, rf, s0f, s2f, u20, u18, d18, mm18, d16, mm16, sl0, sl1, sl2,
-    h0, h2, hs, hg, gf, eb, g22, g20, s4b, mb, pr, ob, dwv, pwv, projv,
+    rin, rf, s0f, s2f, u12, u10, d10, mm10, d8, mm8, sl0, sl1, sl2,
+    h0, h2, hs, hg, gf, eb, g14, g12, s4b, mb, pr, ob, dwv, pwv, projv,
     wsem, xsend, xrecv, rsend, rrecv, osend, orecv, hsend, hrecv,
 ):
     ta, ha, wa = lax.axis_index("ta"), lax.axis_index("ha"), lax.axis_index("wa")
@@ -49,26 +50,33 @@
     def bent(p):
         return jnp.where(p < 2, p, 5 - p)
 
-    def place(a, b):
+    def place(c, a, b):
         p = bent(b)
-        return a * 4 + jnp.where(lax.rem(a, 2) == 0, p, 3 - p)
-
-    row, col = ha * 8 + z, place(ta, low)
+        p = a * 4 + jnp.where(lax.rem(a, 2) == 0, p, 3 - p)
+        return jnp.where(lax.rem(c, 2) == 0, p, 31 - p)
+
+    row, col, line = ha * 4 + lax.div(z, 2), place(z, ta, low), lax.rem(wa, 8)
 
     def at(a, b, c):
         return {"ta": a, "ha": b, "wa": c}
 
     def owner(r, c):
-        a, p = lax.div(c, 4), lax.rem(c, 4)
+        side = lax.div(c, 16)
+        p = jnp.where(side == 0, c, 31 - c)
+        a, p = lax.div(p, 4), lax.rem(p, 4)
         p = bent(jnp.where(lax.rem(a, 2) == 0, p, 3 - p))
-        return at(a, lax.div(r, 8), lax.rem(r, 8) * 4 + p)
+        return at(a, lax.div(r, 4), lax.rem(r, 4) * 8 + side * 4 + p)
+
+    neighbours = {side: owner(row + side[0], col + side[1]) for side in SIDES}
+    fits_row = {-1: row > 0, 0: row >= 0, 1: row < GRID_R - 1}
+    fits_col = {-1: col > 0, 0: col >= 0, 1: col < GRID_C - 1}
+    present = {side: fits_row[side[0]] & fits_col[side[1]] for side in SIDES}
 
     def near(dr, dc):
-        return owner(row + dr, col + dc)
+        return neighbours[dr, dc]
 
     def there(dr, dc):
-        r, c = row + dr, col + dc
-        return (r >= 0) & (r < GRID_R) & (c >= 0) & (c < GRID_C)
+        return present[dr, dc]
 
     weights = []
     for b in range(2):
@@ -83,9 +91,6 @@
         pltpu.make_async_copy(pw, pwv, wsem.at[7]),
         pltpu.make_async_copy(proj, projv, wsem.at[8]),
     ]
-    for copy in small + weights:
-        copy.start()
-
     def clear_outside(buf, k):
         @pl.when(row == 0)
         def _():
@@ -112,73 +117,73 @@
     def greet(device):
         pl.semaphore_signal(barrier, inc=1, device_id=device, device_id_type=MESH)
 
-    spread_count = jnp.where(lax.div(wa, 2) == col, 7, 8)
-    for step in range(8):
-        r = ha * 8 + lax.rem(z + step, 8)
-
-        @pl.when(jnp.logical_not((r == row) & (lax.div(wa, 2) == col)))
-        def _():
-            greet(owner(r, lax.div(wa, 2)))
-
-    for step in range(8):
-        a, b = step // 2, 2 * col + step % 2
-
-        @pl.when(jnp.logical_not((a == ta) & (b == wa)))
-        def _():
-            greet(at(a, ha, b))
-
-    gather_count = jnp.where(lax.div(wa, 2) == col, 7, 8)
-    for step in range(1, 16):
-        greet(owner(row, lax.rem(col + step, 16)))
+    same = wa == col
+    for step in range(4):
+        r = ha * 4 + lax.rem(row + step, 4)
+        if step:
+            greet(owner(r, wa))
+            greet(at(lax.rem(ta + step, 4), ha, col))
+        else:
+            @pl.when(jnp.logical_not(same))
+            def _():
+                greet(owner(r, wa))
+                greet(at(ta, ha, col))
+
+    @pl.loop(1, 32)
+    def _(step):
+        greet(owner(row, lax.rem(col + step, 32)))
+
     near_count = 0
     for dr, dc in SIDES:
-        present = there(dr, dc)
-        near_count = near_count + present.astype(jnp.int32)
-
-        @pl.when(present)
+        near_count = near_count + there(dr, dc).astype(jnp.int32)
+
+        @pl.when(there(dr, dc))
         def _():
             greet(near(dr, dc))
 
-    af[:, :, :, CS:WIDE] = jnp.zeros((TH + 2, TW + 2, 8, WIDE - CS), F32)
-    wb[:, :, :, :, CT:WIDE, :] = jnp.zeros((2, 3, 3, 3, WIDE - CT, CT), BF16)
-    pl.semaphore_wait(barrier, 15 + spread_count + gather_count + near_count)
-
-    own_patch = pltpu.make_async_copy(
-        tin.at[:, pl.ds(z * TH, TH)], xin.at[pl.ds(ta * 2, 2), :, lax.rem(wa, 2)], xrecv
-    )
-    patch_self = lax.div(wa, 2) == col
-    for step in range(8):
-        to = lax.rem(z + step, 8)
+    pl.semaphore_wait(barrier, 39 - 2 * same.astype(jnp.int32) + near_count)
+
+    for step in FAR_FIRST:
+        to = lax.rem(row + step, 4)
+        source, target = tin.at[:, pl.ds(to * TH, TH)], xin.at[pl.ds(ta * 2, 2)]
 
         def send_patch():
             pltpu.make_async_remote_copy(
-                src_ref=tin.at[:, pl.ds(to * TH, TH)],
-                dst_ref=xin.at[pl.ds(ta * 2, 2), :, lax.rem(wa, 2)],
+                src_ref=source,
+                dst_ref=target,
                 send_sem=xsend,
                 recv_sem=xrecv,
-                device_id=owner(ha * 8 + to, lax.div(wa, 2)),
+                device_id=owner(ha * 4 + to, wa),
                 device_id_type=MESH,
             ).start()
 
         if step:
             send_patch()
         else:
-            pl.when(patch_self)(own_patch.start)
-            pl.when(jnp.logical_not(patch_self))(send_patch)
-
-    pltpu.make_async_copy(
-        sin.at[:, pl.ds(col * 2, 2)], rin.at[pl.ds(ta * 2, 2), low], rrecv
-    ).start()
-    for step in range(1, 16):
-        c = lax.rem(col + step, 16)
+            @pl.when(same)
+            def _():
+                pltpu.make_async_copy(source, target, xrecv).start()
+
+            pl.when(jnp.logical_not(same))(send_patch)
+
+    pltpu.make_async_copy(sin.at[:, col], rin.at[pl.ds(ta * 2, 2), line], rrecv).start()
+
+    @pl.loop(1, 32)
+    def _(step):
+        c = lax.rem(col + step, 32)
         pltpu.make_async_remote_copy(
-            src_ref=sin.at[:, pl.ds(c * 2, 2)],
-            dst_ref=rin.at[pl.ds(ta * 2, 2), low],
+            src_ref=sin.at[:, c],
+            dst_ref=rin.at[pl.ds(ta * 2, 2), line],
             send_sem=rsend,
             recv_sem=rrecv,
             device_id=owner(row, c),
             device_id_type=MESH,
         ).start()
+
+    for copy in small + weights:
+        copy.start()
+    af[:, :, :, CS:WIDE] = jnp.zeros((TH + 2, TW + 2, 8, WIDE - CS), F32)
+    wb[:, :, :, :, CT:WIDE, :] = jnp.zeros((2, 3, 3, 3, WIDE - CT, CT), BF16)
 
     def side_copy(buf, k, slot, d):
         dr, dc = SIDES[d]
@@ -267,7 +272,7 @@
             s0f[h + 2, w + 2] = s
             h0[h + 2, w + 2] = s.astype(BF16)
             u, slope = act(s)
-            u20[h + 2, w + 2] = u
+            u12[h + 2, w + 2] = u
             sl0[h, w] = slope
 
     send(h0, 2, 1)
@@ -295,49 +300,47 @@
     def wide_layer(n, field):
         @pl.loop(0, TH + 2)
         def _(h):
-            for w in (0, 9):
-                d18[h, w : w + 9] = taps(u20, h, w, 9, n, False)
-
-        mm18[...] = jnp.dot(
-            d18[...].reshape(864, CS).astype(BF16), pwv[n], preferred_element_type=F32
-        ).reshape(6, 18, 8, CS)
+            d10[h] = taps(u12, h, 0, 10, n, False)
+
+        mm10[...] = jnp.dot(
+            d10[...].reshape(800, CS).astype(BF16), pwv[n], preferred_element_type=F32
+        ).reshape(10, 10, 8, CS)
 
         @pl.loop(0, TH + 2)
         def _(h):
-            s = field[h + 1, 1:19] + mm18[h]
-            mm18[h] = s
+            s = field[h + 1, 1:11] + mm10[h]
+            mm10[h] = s
             u, slope = act(s)
-            u18[h] = u
+            u10[h] = u
             sl1[h] = slope
 
-        clear_outside(u18, 1)
+        clear_outside(u10, 1)
 
     def narrow_layer(n):
         @pl.loop(0, TH)
         def _(h):
-            for w in (0, 8):
-                d16[h, w : w + 8] = taps(u18, h, w, 8, n, False)
-
-        mm16[...] = jnp.dot(
-            d16[...].reshape(512, CS).astype(BF16), pwv[n], preferred_element_type=F32
-        ).reshape(4, 16, 8, CS)
+            d8[h] = taps(u10, h, 0, 8, n, False)
+
+        mm8[...] = jnp.dot(
+            d8[...].reshape(512, CS).astype(BF16), pwv[n], preferred_element_type=F32
+        ).reshape(8, 8, 8, CS)
 
     receive(h0, 2, 1)
     for rows, cols in ring(2):
         s = h0[rows, cols].astype(F32)
         s0f[rows, cols] = s
-        u20[rows, cols] = act(s)[0]
+        u12[rows, cols] = act(s)[0]
     wide_layer(0, s0f)
     narrow_layer(1)
 
     @pl.loop(0, TH)
     def _(h):
-        s = mm18[h + 1, 1:17] + mm16[h]
-        s2f[h + 2, 2:18] = s
-        h2[h + 2, 2:18] = s.astype(BF16)
+        s = mm10[h + 1, 1:9] + mm8[h]
+        s2f[h + 2, 2:10] = s
+        h2[h + 2, 2:10] = s.astype(BF16)
         u, slope = act(s)
-        u20[h + 2, 2:18] = u
-        sl2[h + 2, 2:18] = slope
+        u12[h + 2, 2:10] = u
+        sl2[h + 2, 2:10] = slope
 
     send(h2, 2, 3)
 
@@ -348,10 +351,9 @@
 
     @pl.loop(0, 8)
     def _(m):
-        h, w = lax.div(m, 2), lax.rem(m, 2) * 8
         a = silu_norm(conv_row(m))
-        hsec[h + 1, pl.ds(w + 1, 8)] = a.astype(BF16)
-        af[h + 1, pl.ds(w + 1, 8), :, 0:CT] = a
+        hsec[m + 1, 1:9] = a.astype(BF16)
+        af[m + 1, 1:9, :, 0:CT] = a
 
     send(hsec, 1, 2)
 
@@ -360,31 +362,30 @@
         s = h2[rows, cols].astype(F32)
         s2f[rows, cols] = s
         u, slope = act(s)
-        u20[rows, cols] = u
+        u12[rows, cols] = u
         sl2[rows, cols] = slope
 
     @pl.loop(0, TH + 2)
     def _(h):
-        for w in (0, 9):
-            d18[h, w : w + 9] = taps(u20, h, w, 9, 2, False)
-
-    mm18[...] = jnp.dot(
-        d18[...].reshape(864, CS).astype(BF16), pwv[2], preferred_element_type=F32
-    ).reshape(6, 18, 8, CS)
+        d10[h] = taps(u12, h, 0, 10, 2, False)
+
+    mm10[...] = jnp.dot(
+        d10[...].reshape(800, CS).astype(BF16), pwv[2], preferred_element_type=F32
+    ).reshape(10, 10, 8, CS)
 
     @pl.loop(0, TH + 2)
     def _(h):
-        s = s2f[h + 1, 1:19] + mm18[h]
-        mm18[h] = s
+        s = s2f[h + 1, 1:11] + mm10[h]
+        mm10[h] = s
         u, slope = act(s)
-        u18[h] = u
-        d18[h] = slope
-
-    hs[3:7, 3:19] = d18[1:5, 1:17].astype(BF16)
+        u10[h] = u
+        d10[h] = slope
+
+    hs[3:11, 3:11] = d10[1:9, 1:9].astype(BF16)
     send(hs, 3, 4)
-    clear_outside(u18, 1)
+    clear_outside(u10, 1)
     narrow_layer(3)
-    s4b[...] = (mm18[1:5, 1:17] + mm16[...]).reshape(512, CS).astype(BF16)
+    s4b[...] = (mm10[1:9, 1:9] + mm8[...]).reshape(512, CS).astype(BF16)
 
     pr[...] = lax.dot_general(s4b[...], projv[...], TRANSPOSED, preferred_element_type=F32)
 
@@ -395,14 +396,13 @@
 
     @pl.loop(0, 8)
     def _(m):
-        h, w = lax.div(m, 2), lax.rem(m, 2) * 8
-        target = (xt[h, pl.ds(w, 8)] + conv_row(m)).reshape(64, CT)
+        target = (xt[m] + conv_row(m)).reshape(64, CT)
         span = pl.ds(m * 64, 64)
         mb[span] = (pr[span] - target).astype(BF16)
 
-    g = jnp.dot(mb[...], projv[...], preferred_element_type=F32).reshape(4, 16, 8, CS)
-    gf[4:8, 4:20] = g
-    hg[4:8, 4:20] = g.astype(BF16)
+    g = jnp.dot(mb[...], projv[...], preferred_element_type=F32).reshape(8, 8, 8, CS)
+    gf[4:12, 4:12] = g
+    hg[4:12, 4:12] = g.astype(BF16)
     send(hg, 4, 5)
 
     receive(hs, 3, 4)
@@ -421,84 +421,77 @@
 
     back(3, gf, 4)
 
+    @pl.loop(0, 14)
+    def _(h):
+        for w in (0, 7):
+            slope = hs[h, w : w + 7].astype(F32)
+            g14[h, w : w + 7] = (
+                gf[h + 1, w + 1 : w + 8] + taps(eb, h, w, 7, 3, True) * slope
+            )
+
+    clear_outside(g14, 3)
+    back(2, g14, 3)
+
+    @pl.loop(0, 12)
+    def _(h):
+        for w in (0, 6):
+            g12[h, w : w + 6] = (
+                g14[h + 1, w + 1 : w + 7]
+                + taps(eb, h, w, 6, 2, True) * sl2[h, w : w + 6]
+            )
+
+    clear_outside(g12, 2)
+    back(1, g12, 2)
+
     @pl.loop(0, 10)
     def _(h):
-        for w in (0, 11):
-            slope = hs[h, w : w + 11].astype(F32)
-            g22[h, w : w + 11] = (
-                gf[h + 1, w + 1 : w + 12] + taps(eb, h, w, 11, 3, True) * slope
-            )
-
-    clear_outside(g22, 3)
-    back(2, g22, 3)
-
-    @pl.loop(0, 8)
-    def _(h):
-        for w in (0, 10):
-            g20[h, w : w + 10] = (
-                g22[h + 1, w + 1 : w + 11]
-                + taps(eb, h, w, 10, 2, True) * sl2[h, w : w + 10]
-            )
-
-    clear_outside(g20, 2)
-    back(1, g20, 2)
-
-    @pl.loop(0, 6)
-    def _(h):
-        for w in (0, 9):
-            d18[h, w : w + 9] = (
-                g20[h + 1, w + 1 : w + 10]
-                + taps(eb, h, w, 9, 1, True) * sl1[h, w : w + 9]
-            )
-
-    clear_outside(d18, 1)
-    back(0, d18, 1)
-
-    @pl.loop(0, 4)
-    def _(h):
-        for w in (0, 8):
-            g = (
-                d18[h + 1, w + 1 : w + 9]
-                + taps(eb, h, w, 8, 0, True) * sl0[h, w : w + 8]
-            )
-            rf[pl.ds(h * 128 + w * 8, 64)] = g.reshape(64, CS)
+        d10[h] = g12[h + 1, 1:11] + taps(eb, h, 0, 10, 1, True) * sl1[h]
+
+    clear_outside(d10, 1)
+    back(0, d10, 1)
+
+    def send_back(x, h):
+        pltpu.make_async_remote_copy(
+            src_ref=ob.at[pl.ds(x * 2, 2), h],
+            dst_ref=out.at[:, col],
+            send_sem=osend,
+            recv_sem=orecv,
+            device_id=at(x, ha, wa - line + h),
+            device_id_type=MESH,
+        ).start()
 
     @pl.loop(0, TH)
     def _(h):
-        for half in range(2):
-            for t in range(8):
-                ob[t, h, half] = rf[
-                    pl.ds(h * 128 + half * 64 + t, 8, stride=8), :
-                ].astype(BF16)
-
-    for step in range(16):
-        x, y = lax.rem(ta + step // 4, 4), lax.rem(low + step % 4, 4)
-        source = ob.at[pl.ds(x * 2, 2), y]
-        if step:
-            pltpu.make_async_remote_copy(
-                src_ref=source,
-                dst_ref=out.at[:, pl.ds(col * 2, 2)],
-                send_sem=osend,
-                recv_sem=orecv,
-                device_id=at(x, ha, z * 4 + y),
-                device_id_type=MESH,
+        g = d10[h + 1, 1:9] + taps(eb, h, 0, 8, 0, True) * sl0[h]
+        rf[pl.ds(h * 64, 64)] = g.reshape(64, CS)
+        for t in range(8):
+            ob[t, h] = rf[pl.ds(h * 64 + t, 8, stride=8), :].astype(BF16)
+        for step in (2, 1, 3):
+            send_back(lax.rem(ta + step, 4), h)
+
+        @pl.when(h == line)
+        def _():
+            pltpu.make_async_copy(
+                ob.at[pl.ds(ta * 2, 2), h], out.at[:, col], orecv
             ).start()
-        else:
-            pltpu.make_async_copy(source, out.at[:, pl.ds(col * 2, 2)], orecv).start()
+
+        @pl.when(h != line)
+        def _():
+            send_back(ta, h)
 
     for buf, k, slot in halos:
         drain(buf, k, slot)
 
-    @pl.when(patch_self)
+    @pl.when(same)
     def _():
-        part = tin.at[:, 0:28]
+        part = tin.at[:, 0:24]
         pltpu.make_async_copy(part, part, xsend).wait()
 
-    @pl.when(jnp.logical_not(patch_self))
+    @pl.when(jnp.logical_not(same))
     def _():
         pltpu.make_async_copy(tin, tin, xsend).wait()
 
-    part = sin.at[:, 0:30]
+    part = sin.at[:, 0:31]
     pltpu.make_async_copy(part, part, rsend).wait()
     pltpu.make_async_copy(part, part, osend).wait()
     pltpu.make_async_copy(out, out, orecv).wait()
@@ -512,7 +505,7 @@
         return pltpu.VMEM((TH + 2 * k, TW + 2 * k, 8, c), kind)
 
     scratch = [
-        pltpu.VMEM((8, TH, 2, 8, CT), BF16),
+        pltpu.VMEM((8, 8, 8, CT), BF16),
         pltpu.VMEM((2, 512, CS), F32),
         tile(0, CT, F32),
         tile(1, CT, BF16),
@@ -521,7 +514,7 @@
         pltpu.VMEM((512, 9 * WIDE), BF16),
         pltpu.VMEM((2, 3, 3, 3, WIDE, CT), BF16),
         pltpu.VMEM((3, 512, CT), F32),
-        pltpu.VMEM((8, TH, 2, 8, CS), BF16),
+        pltpu.VMEM((8, 8, 8, CS), BF16),
         pltpu.VMEM((512, CS), F32),
         tile(2, CS, F32),
         tile(2, CS, F32),
@@ -545,7 +538,7 @@
         pltpu.VMEM((512, CS), BF16),
         pltpu.VMEM((512, CT), BF16),
         pltpu.VMEM((512, CT), F32),
-        pltpu.VMEM((8, TH, 2, 8, CS), BF16),
+        pltpu.VMEM((8, 8, 8, CS), BF16),
         pltpu.VMEM((3, 3, 3, 4, CS), F32),
         pltpu.VMEM((4, CS, CS), BF16),
         pltpu.VMEM((CT, CS), BF16),

time: 74.9 us -> 73.6 us (0.983)
  Pallas kernels: 73.2 us -> 71.3 us
    pallas_call x1, Pallas kernels: 73.2 us -> 71.3 us  [on_device(): pl.pallas_call(kernel, out_shape=jax.ShapeDtypeStruct((2, 32, 8, CS), BF1...]
where the time goes in v3:
time: 73.6 us; the launch traced here: 72.9 us
  Pallas kernels  71.3 us (97%)
  local copies, waits for them, and re-layouts  1.57 us (2%)
    pallas_call x1, Pallas kernels, on_device(): pl.pallas_call(kernel, out_shape=jax.ShapeDtypeStruct((2, 32, 8, CS), BF1...  71.3 us
    unnamed x1, local copies, waits for them, and re-layouts  1.57 us

profile of v3, /device:TPU:57, one launch (start us, length us, event | category | flops | bytes accessed | tf_op | source)
XLA Modules:
  0.0 72.9 jit_solution(5172451475134185576)
XLA Ops:
  0.0 71.3 %shard_map.64 = bf16[2,32,8,128]{3,2,1,0:T(8,128)(2,1)} custom-call(bf16[2,32,8,192]{3,2,1,0:T(8,128)(2,1)} %tin.1, bf16[1,2,3,3,3,192,192]{6,5,4,3,2,1,0:T(8,128)(2,1)} %tw.1, bf16[2,32,8,128]{3,2,1,0:T(8,128)(2,1)} %bitcast.7, f32[3,3,3,4,128]{4,3,2,1,0:T(4,128)} %bitcast.8, bf16[4,128,128]{2,1,0:T(8,128)(2,1)} %pw.1, bf16[192,128]{1,0:T(8,128)(2,1)} %bitcast.9), custom_call_target="tpu_custom_call" | custom-call | tf_op jit(solution)/shard_map/pallas_call | solution.py:555
  71.3 1.6 %copy.9 = bf16[2,1,256,128]{3,2,1,0:T(8,128)(2,1)} copy(bf16[2,1,256,128]{3,2,1,0:T(8,128)(2,1)} %bitcast.6) | data formatting | bytes 262144

commit v4 on v2

--- a/solution.py
+++ b/solution.py
@@ -7,7 +7,8 @@
 
 MESH = pl.DeviceIdType.MESH
 F32, BF16 = jnp.float32, jnp.bfloat16
-SIDES = [(0, -1), (0, 1), (-1, 0), (1, 0), (-1, -1), (-1, 1), (1, -1), (1, 1)]
+SIDES = [(-1, 0), (1, 0), (-1, -1), (-1, 1), (1, -1), (1, 1), (0, -1), (0, 1)]
+FAR_FIRST = (4, 3, 5, 2, 6, 1, 7, 0)
 CT, CS, WIDE = 192, 128, 256
 TH, TW = 4, 16
 GRID_R, GRID_C = 32, 16
@@ -53,7 +54,10 @@
         p = bent(b)
         return a * 4 + jnp.where(lax.rem(a, 2) == 0, p, 3 - p)
 
-    row, col = ha * 8 + z, place(ta, low)
+    upper = lax.div(low, 2)
+    spot, col = lax.rem(z + 8 - upper, 8), place(ta, low)
+    row, held = ha * 8 + spot, ha * 8 + z
+    first = upper == 0
 
     def at(a, b, c):
         return {"ta": a, "ha": b, "wa": c}
@@ -61,14 +65,18 @@
     def owner(r, c):
         a, p = lax.div(c, 4), lax.rem(c, 4)
         p = bent(jnp.where(lax.rem(a, 2) == 0, p, 3 - p))
-        return at(a, lax.div(r, 8), lax.rem(r, 8) * 4 + p)
+        return at(a, lax.div(r, 8), lax.rem(lax.rem(r, 8) + lax.div(p, 2), 8) * 4 + p)
+
+    neighbours = {side: owner(row + side[0], col + side[1]) for side in SIDES}
+    fits_row = {-1: row > 0, 0: row >= 0, 1: row < GRID_R - 1}
+    fits_col = {-1: col > 0, 0: col >= 0, 1: col < GRID_C - 1}
+    present = {side: fits_row[side[0]] & fits_col[side[1]] for side in SIDES}
 
     def near(dr, dc):
-        return owner(row + dr, col + dc)
+        return neighbours[dr, dc]
 
     def there(dr, dc):
-        r, c = row + dr, col + dc
-        return (r >= 0) & (r < GRID_R) & (c >= 0) & (c < GRID_C)
+        return present[dr, dc]
 
     weights = []
     for b in range(2):
@@ -83,9 +91,6 @@
         pltpu.make_async_copy(pw, pwv, wsem.at[7]),
         pltpu.make_async_copy(proj, projv, wsem.at[8]),
     ]
-    for copy in small + weights:
-        copy.start()
-
     def clear_outside(buf, k):
         @pl.when(row == 0)
         def _():
@@ -112,73 +117,96 @@
     def greet(device):
         pl.semaphore_signal(barrier, inc=1, device_id=device, device_id_type=MESH)
 
-    spread_count = jnp.where(lax.div(wa, 2) == col, 7, 8)
-    for step in range(8):
-        r = ha * 8 + lax.rem(z + step, 8)
-
-        @pl.when(jnp.logical_not((r == row) & (lax.div(wa, 2) == col)))
-        def _():
-            greet(owner(r, lax.div(wa, 2)))
-
-    for step in range(8):
-        a, b = step // 2, 2 * col + step % 2
+    block = lax.div(wa, 2)
+    same = block == col
+
+    @pl.loop(0, 8)
+    def _(step):
+        r = ha * 8 + lax.rem(spot + step, 8)
+
+        @pl.when(jnp.logical_not((step == 0) & same))
+        def _():
+            greet(owner(r, block))
+
+        a, b = lax.div(step, 2), 2 * col + lax.rem(step, 2)
 
         @pl.when(jnp.logical_not((a == ta) & (b == wa)))
         def _():
             greet(at(a, ha, b))
 
-    gather_count = jnp.where(lax.div(wa, 2) == col, 7, 8)
-    for step in range(1, 16):
-        greet(owner(row, lax.rem(col + step, 16)))
+    @pl.loop(0, 16)
+    def _(step):
+        @pl.when(jnp.logical_not(first & (step == 0)))
+        def _():
+            greet(owner(held, lax.rem(col + step, 16)))
+
+        x, y = lax.div(step, 4), lax.rem(step, 4)
+
+        @pl.when(jnp.logical_not(first & (x == ta) & (y == low)))
+        def _():
+            greet(at(x, ha, spot * 4 + y))
+
     near_count = 0
     for dr, dc in SIDES:
-        present = there(dr, dc)
-        near_count = near_count + present.astype(jnp.int32)
-
-        @pl.when(present)
+        near_count = near_count + there(dr, dc).astype(jnp.int32)
+
+        @pl.when(there(dr, dc))
         def _():
             greet(near(dr, dc))
 
-    af[:, :, :, CS:WIDE] = jnp.zeros((TH + 2, TW + 2, 8, WIDE - CS), F32)
-    wb[:, :, :, :, CT:WIDE, :] = jnp.zeros((2, 3, 3, 3, WIDE - CT, CT), BF16)
-    pl.semaphore_wait(barrier, 15 + spread_count + gather_count + near_count)
-
-    own_patch = pltpu.make_async_copy(
-        tin.at[:, pl.ds(z * TH, TH)], xin.at[pl.ds(ta * 2, 2), :, lax.rem(wa, 2)], xrecv
+    pl.semaphore_wait(
+        barrier, 48 - 2 * same.astype(jnp.int32) - 2 * first.astype(jnp.int32) + near_count
     )
-    patch_self = lax.div(wa, 2) == col
-    for step in range(8):
-        to = lax.rem(z + step, 8)
+
+    for step in FAR_FIRST:
+        to = lax.rem(spot + step, 8)
+        source = tin.at[:, pl.ds(to * TH, TH)]
+        target = xin.at[pl.ds(ta * 2, 2), :, lax.rem(wa, 2)]
 
         def send_patch():
             pltpu.make_async_remote_copy(
-                src_ref=tin.at[:, pl.ds(to * TH, TH)],
-                dst_ref=xin.at[pl.ds(ta * 2, 2), :, lax.rem(wa, 2)],
+                src_ref=source,
+                dst_ref=target,
                 send_sem=xsend,
                 recv_sem=xrecv,
-                device_id=owner(ha * 8 + to, lax.div(wa, 2)),
+                device_id=owner(ha * 8 + to, block),
                 device_id_type=MESH,
             ).start()
 
         if step:
             send_patch()
         else:
-            pl.when(patch_self)(own_patch.start)
-            pl.when(jnp.logical_not(patch_self))(send_patch)
-
-    pltpu.make_async_copy(
-        sin.at[:, pl.ds(col * 2, 2)], rin.at[pl.ds(ta * 2, 2), low], rrecv
-    ).start()
-    for step in range(1, 16):
+            @pl.when(same)
+            def _():
+                pltpu.make_async_copy(source, target, xrecv).start()
+
+            pl.when(jnp.logical_not(same))(send_patch)
+
+    @pl.loop(0, 16)
+    def _(step):
         c = lax.rem(col + step, 16)
-        pltpu.make_async_remote_copy(
-            src_ref=sin.at[:, pl.ds(c * 2, 2)],
-            dst_ref=rin.at[pl.ds(ta * 2, 2), low],
-            send_sem=rsend,
-            recv_sem=rrecv,
-            device_id=owner(row, c),
-            device_id_type=MESH,
-        ).start()
+        source, target = sin.at[:, pl.ds(c * 2, 2)], rin.at[pl.ds(ta * 2, 2), low]
+        itself = first & (step == 0)
+
+        @pl.when(itself)
+        def _():
+            pltpu.make_async_copy(source, target, rrecv).start()
+
+        @pl.when(jnp.logical_not(itself))
+        def _():
+            pltpu.make_async_remote_copy(
+                src_ref=source,
+                dst_ref=target,
+                send_sem=rsend,
+                recv_sem=rrecv,
+                device_id=owner(held, c),
+                device_id_type=MESH,
+            ).start()
+
+    for copy in small + weights:
+        copy.start()
+    af[:, :, :, CS:WIDE] = jnp.zeros((TH + 2, TW + 2, 8, WIDE - CS), F32)
+    wb[:, :, :, :, CT:WIDE, :] = jnp.zeros((2, 3, 3, 3, WIDE - CT, CT), BF16)
 
     def side_copy(buf, k, slot, d):
         dr, dc = SIDES[d]
@@ -454,7 +482,17 @@
     clear_outside(d18, 1)
     back(0, d18, 1)
 
-    @pl.loop(0, 4)
+    def send_back(x, h):
+        pltpu.make_async_remote_copy(
+            src_ref=ob.at[pl.ds(x * 2, 2), h],
+            dst_ref=out.at[:, pl.ds(col * 2, 2)],
+            send_sem=osend,
+            recv_sem=orecv,
+            device_id=at(x, ha, spot * 4 + h),
+            device_id_type=MESH,
+        ).start()
+
+    @pl.loop(0, TH)
     def _(h):
         for w in (0, 8):
             g = (
@@ -462,45 +500,46 @@
                 + taps(eb, h, w, 8, 0, True) * sl0[h, w : w + 8]
             )
             rf[pl.ds(h * 128 + w * 8, 64)] = g.reshape(64, CS)
-
-    @pl.loop(0, TH)
-    def _(h):
         for half in range(2):
             for t in range(8):
                 ob[t, h, half] = rf[
                     pl.ds(h * 128 + half * 64 + t, 8, stride=8), :
                 ].astype(BF16)
-
-    for step in range(16):
-        x, y = lax.rem(ta + step // 4, 4), lax.rem(low + step % 4, 4)
-        source = ob.at[pl.ds(x * 2, 2), y]
-        if step:
-            pltpu.make_async_remote_copy(
-                src_ref=source,
-                dst_ref=out.at[:, pl.ds(col * 2, 2)],
-                send_sem=osend,
-                recv_sem=orecv,
-                device_id=at(x, ha, z * 4 + y),
-                device_id_type=MESH,
+        for step in (2, 1, 3):
+            send_back(lax.rem(ta + step, 4), h)
+
+        @pl.when(first & (h == low))
+        def _():
+            pltpu.make_async_copy(
+                ob.at[pl.ds(ta * 2, 2), h], out.at[:, pl.ds(col * 2, 2)], orecv
             ).start()
-        else:
-            pltpu.make_async_copy(source, out.at[:, pl.ds(col * 2, 2)], orecv).start()
+
+        @pl.when(jnp.logical_not(first & (h == low)))
+        def _():
+            send_back(ta, h)
 
     for buf, k, slot in halos:
         drain(buf, k, slot)
 
-    @pl.when(patch_self)
+    @pl.when(same)
     def _():
         part = tin.at[:, 0:28]
         pltpu.make_async_copy(part, part, xsend).wait()
 
-    @pl.when(jnp.logical_not(patch_self))
+    @pl.when(jnp.logical_not(same))
     def _():
         pltpu.make_async_copy(tin, tin, xsend).wait()
 
-    part = sin.at[:, 0:30]
-    pltpu.make_async_copy(part, part, rsend).wait()
-    pltpu.make_async_copy(part, part, osend).wait()
+    for sem in (rsend, osend):
+        @pl.when(first)
+        def _():
+            part = sin.at[:, 0:30]
+            pltpu.make_async_copy(part, part, sem).wait()
+
+        @pl.when(jnp.logical_not(first))
+        def _():
+            pltpu.make_async_copy(sin, sin, sem).wait()
+
     pltpu.make_async_copy(out, out, orecv).wait()
 
 

time: 74.9 us -> 71 us (0.948)
  Pallas kernels: 73.2 us -> 69.3 us
    pallas_call x1, Pallas kernels: 73.2 us -> 69.3 us  [on_device(): pl.pallas_call(kernel, out_shape=jax.ShapeDtypeStruct((2, 32, 8, CS), BF1...]
where the time goes in v4:
time: 71 us; the launch traced here: 70.9 us
  Pallas kernels  69.3 us (98%)
  local copies, waits for them, and re-layouts  1.57 us (2%)
    pallas_call x1, Pallas kernels, on_device(): pl.pallas_call(kernel, out_shape=jax.ShapeDtypeStruct((2, 32, 8, CS), BF1...  69.3 us
    unnamed x1, local copies, waits for them, and re-layouts  1.57 us

profile of v4, /device:TPU:57, one launch (start us, length us, event | category | flops | bytes accessed | tf_op | source)
XLA Modules:
  0.0 70.9 jit_solution(10062847462587218958)
XLA Ops:
  0.0 69.3 %shard_map.64 = bf16[2,32,8,128]{3,2,1,0:T(8,128)(2,1)} custom-call(bf16[2,32,8,192]{3,2,1,0:T(8,128)(2,1)} %tin.1, bf16[1,2,3,3,3,192,192]{6,5,4,3,2,1,0:T(8,128)(2,1)} %tw.1, bf16[2,32,8,128]{3,2,1,0:T(8,128)(2,1)} %bitcast.7, f32[3,3,3,4,128]{4,3,2,1,0:T(4,128)} %bitcast.8, bf16[4,128,128]{2,1,0:T(8,128)(2,1)} %pw.1, bf16[192,128]{1,0:T(8,128)(2,1)} %bitcast.9), custom_call_target="tpu_custom_call" | custom-call | tf_op jit(solution)/shard_map/pallas_call | solution.py:601
  69.3 1.6 %copy.9 = bf16[2,1,256,128]{3,2,1,0:T(8,128)(2,1)} copy(bf16[2,1,256,128]{3,2,1,0:T(8,128)(2,1)} %bitcast.6) | data formatting | bytes 262144

commit v5 on v4

--- a/solution.py
+++ b/solution.py
@@ -41,7 +41,7 @@
     tin, tw, sin, dw, pw, proj, out,
     xin, xf, xt, hact, hsec, af, lhs, wb, pp,
     rin, rf, s0f, s2f, u20, u18, d18, mm18, d16, mm16, sl0, sl1, sl2,
-    h0, h2, hs, hg, gf, eb, g22, g20, s4b, mb, pr, ob, dwv, pwv, projv,
+    h0, h2, hs, hg, gf, eb, pa, pb, kb, g22, g20, s4b, mb, pr, ob, dwv, pwv, projv,
     wsem, xsend, xrecv, rsend, rrecv, osend, orecv, hsend, hrecv,
 ):
     ta, ha, wa = lax.axis_index("ta"), lax.axis_index("ha"), lax.axis_index("wa")
@@ -134,17 +134,15 @@
         def _():
             greet(at(a, ha, b))
 
-    @pl.loop(0, 16)
-    def _(step):
-        @pl.when(jnp.logical_not(first & (step == 0)))
-        def _():
-            greet(owner(held, lax.rem(col + step, 16)))
-
-        x, y = lax.div(step, 4), lax.rem(step, 4)
-
-        @pl.when(jnp.logical_not(first & (x == ta) & (y == low)))
-        def _():
-            greet(at(x, ha, spot * 4 + y))
+    planes = [z * 4, lax.rem(z + 1, 8) * 4]
+    for a in range(4):
+        for b in range(4):
+            itself = first & (a == ta) & (b == low)
+
+            @pl.when(jnp.logical_not(itself))
+            def _():
+                greet(at(a, ha, planes[b // 2] + b))
+                greet(at(a, ha, spot * 4 + b))
 
     near_count = 0
     for dr, dc in SIDES:
@@ -256,17 +254,28 @@
     frames = lax.broadcasted_iota(jnp.int32, (1, 8, CS), 1)
     wide_frames = lax.broadcasted_iota(jnp.int32, (1, 8, CT), 1)
 
-    def taps(src, h, start, width, n, flip):
+    def taps(src, h, start, width, n):
         acc = [None] * 3
         for j in range(3):
             for l in range(3):
                 x = src[h + j, start + l : start + l + width]
                 for i in range(3):
-                    jj, ll = (2 - j, 2 - l) if flip else (j, l)
-                    term = x * dwv[i, jj, ll, n : n + 1, :].reshape(1, 1, CS)
+                    term = x * dwv[i, j, l, n : n + 1, :].reshape(1, 1, CS)
                     acc[i] = term if acc[i] is None else acc[i] + term
-        sign = -1 if flip else 1
-        return acc[2] + shifted(acc[1], sign, frames) + shifted(acc[0], 2 * sign, frames)
+        return acc[2] + shifted(acc[1], 1, frames) + shifted(acc[0], 2, frames)
+
+    def taps_back(h, start, pairs, n):
+        acc = [None] * 3
+        for j in range(3):
+            for l in range(3):
+                held_at = pb if l == 1 else pa
+                first_pair = start + l // 2
+                x = held_at[h + j, first_pair : first_pair + pairs]
+                for i in range(3):
+                    term = x * kb[n, i, 2 - j, 2 - l]
+                    acc[i] = term if acc[i] is None else acc[i] + term
+        acc = [a.astype(F32).reshape(2 * pairs, 8, CS) for a in acc]
+        return acc[2] + shifted(acc[1], -1, frames) + shifted(acc[0], -2, frames)
 
     def conv(b):
         for j in range(3):
@@ -285,6 +294,16 @@
         p = [pp[i, pl.ds(m * 64, 64)].reshape(8, 8, CT) for i in range(3)]
         return p[2] + shifted(p[1], 1, wide_frames) + shifted(p[0], 2, wide_frames)
 
+    for copy in small:
+        copy.wait()
+    for n in range(4):
+        for i in range(3):
+            for j in range(3):
+                for l in range(3):
+                    kb[n, i, j, l] = jnp.broadcast_to(
+                        dwv[i, j, l, n : n + 1, :], (16, CS)
+                    ).astype(BF16)
+
     pltpu.make_async_copy(rin, rin, rrecv).wait()
     rf[...] = rin[...].astype(F32).reshape(512, CS)
 
@@ -317,14 +336,11 @@
 
     send(hact, 1, 0)
 
-    for copy in small:
-        copy.wait()
-
     def wide_layer(n, field):
         @pl.loop(0, TH + 2)
         def _(h):
             for w in (0, 9):
-                d18[h, w : w + 9] = taps(u20, h, w, 9, n, False)
+                d18[h, w : w + 9] = taps(u20, h, w, 9, n)
 
         mm18[...] = jnp.dot(
             d18[...].reshape(864, CS).astype(BF16), pwv[n], preferred_element_type=F32
@@ -344,7 +360,7 @@
         @pl.loop(0, TH)
         def _(h):
             for w in (0, 8):
-                d16[h, w : w + 8] = taps(u18, h, w, 8, n, False)
+                d16[h, w : w + 8] = taps(u18, h, w, 8, n)
 
         mm16[...] = jnp.dot(
             d16[...].reshape(512, CS).astype(BF16), pwv[n], preferred_element_type=F32
@@ -394,7 +410,7 @@
     @pl.loop(0, TH + 2)
     def _(h):
         for w in (0, 9):
-            d18[h, w : w + 9] = taps(u20, h, w, 9, 2, False)
+            d18[h, w : w + 9] = taps(u20, h, w, 9, 2)
 
     mm18[...] = jnp.dot(
         d18[...].reshape(864, CS).astype(BF16), pwv[2], preferred_element_type=F32
@@ -446,38 +462,33 @@
             TRANSPOSED,
             preferred_element_type=F32,
         ).reshape(rows, cols, 8, CS)
+        half = cols // 2
+
+        @pl.loop(0, rows)
+        def _(h):
+            pa[h, 0:half] = eb[h, 0:cols].reshape(half, 16, CS).astype(BF16)
+            pb[h, 0 : half - 1] = eb[h, 1 : cols - 1].reshape(half - 1, 16, CS).astype(BF16)
 
     back(3, gf, 4)
 
     @pl.loop(0, 10)
     def _(h):
-        for w in (0, 11):
-            slope = hs[h, w : w + 11].astype(F32)
-            g22[h, w : w + 11] = (
-                gf[h + 1, w + 1 : w + 12] + taps(eb, h, w, 11, 3, True) * slope
-            )
+        slope = hs[h].astype(F32)
+        g22[h] = gf[h + 1, 1:23] + taps_back(h, 0, 11, 3) * slope
 
     clear_outside(g22, 3)
     back(2, g22, 3)
 
     @pl.loop(0, 8)
     def _(h):
-        for w in (0, 10):
-            g20[h, w : w + 10] = (
-                g22[h + 1, w + 1 : w + 11]
-                + taps(eb, h, w, 10, 2, True) * sl2[h, w : w + 10]
-            )
+        g20[h] = g22[h + 1, 1:21] + taps_back(h, 0, 10, 2) * sl2[h]
 
     clear_outside(g20, 2)
     back(1, g20, 2)
 
     @pl.loop(0, 6)
     def _(h):
-        for w in (0, 9):
-            d18[h, w : w + 9] = (
-                g20[h + 1, w + 1 : w + 10]
-                + taps(eb, h, w, 9, 1, True) * sl1[h, w : w + 9]
-            )
+        d18[h] = g20[h + 1, 1:19] + taps_back(h, 0, 9, 1) * sl1[h]
 
     clear_outside(d18, 1)
     back(0, d18, 1)
@@ -494,12 +505,8 @@
 
     @pl.loop(0, TH)
     def _(h):
-        for w in (0, 8):
-            g = (
-                d18[h + 1, w + 1 : w + 9]
-                + taps(eb, h, w, 8, 0, True) * sl0[h, w : w + 8]
-            )
-            rf[pl.ds(h * 128 + w * 8, 64)] = g.reshape(64, CS)
+        g = d18[h + 1, 1:17] + taps_back(h, 0, 8, 0) * sl0[h]
+        rf[pl.ds(h * 128, 128)] = g.reshape(128, CS)
         for half in range(2):
             for t in range(8):
                 ob[t, h, half] = rf[
@@ -579,6 +586,9 @@
         tile(4, CS, BF16),
         tile(4, CS, F32),
         tile(4, CS, F32),
+        pltpu.VMEM((12, 12, 16, CS), BF16),
+        pltpu.VMEM((12, 11, 16, CS), BF16),
+        pltpu.VMEM((4, 3, 3, 3, 16, CS), BF16),
         tile(3, CS, F32),
         tile(2, CS, F32),
         pltpu.VMEM((512, CS), BF16),

time: 71 us -> 72 us (1.014)
  Pallas kernels: 69.3 us -> 70.3 us
    pallas_call x1, Pallas kernels: 69.3 us -> 70.3 us  [on_device(): pl.pallas_call(kernel, out_shape=jax.ShapeDtypeStruct((2, 32, 8, CS), BF1...]
where the time goes in v5:
time: 72 us; the launch traced here: 71.8 us
  Pallas kernels  70.3 us (98%)
  local copies, waits for them, and re-layouts  1.57 us (2%)
    pallas_call x1, Pallas kernels, on_device(): pl.pallas_call(kernel, out_shape=jax.ShapeDtypeStruct((2, 32, 8, CS), BF1...  70.3 us
    unnamed x1, local copies, waits for them, and re-layouts  1.57 us

profile of v5, /device:TPU:57, one launch (start us, length us, event | category | flops | bytes accessed | tf_op | source)
XLA Modules:
  0.0 71.8 jit_solution(7609693525637964644)
XLA Ops:
  0.0 70.3 %shard_map.64 = bf16[2,32,8,128]{3,2,1,0:T(8,128)(2,1)} custom-call(bf16[2,32,8,192]{3,2,1,0:T(8,128)(2,1)} %tin.1, bf16[1,2,3,3,3,192,192]{6,5,4,3,2,1,0:T(8,128)(2,1)} %tw.1, bf16[2,32,8,128]{3,2,1,0:T(8,128)(2,1)} %bitcast.7, f32[3,3,3,4,128]{4,3,2,1,0:T(4,128)} %bitcast.8, bf16[4,128,128]{2,1,0:T(8,128)(2,1)} %pw.1, bf16[192,128]{1,0:T(8,128)(2,1)} %bitcast.9), custom_call_target="tpu_custom_call" | custom-call | tf_op jit(solution)/shard_map/pallas_call | solution.py:611
  70.3 1.6 %copy.9 = bf16[2,1,256,128]{3,2,1,0:T(8,128)(2,1)} copy(bf16[2,1,256,128]{3,2,1,0:T(8,128)(2,1)} %bitcast.6) | data formatting | bytes 262144

commit v6 on v4

--- a/solution.py
+++ b/solution.py
@@ -108,8 +108,8 @@
         def _():
             buf[:, TW + k :] = jnp.zeros_like(buf[:, TW + k :])
 
-    halos = ((hact, 1, 0), (h0, 2, 1), (hsec, 1, 2), (h2, 2, 3), (hs, 3, 4), (hg, 4, 5))
-    for buf, k, _ in halos:
+    halos = ((hact, 1, 0), (h0, 2, 1), (hsec, 1, 2), (h2, 2, 3), (hs, 3, 4), (hg, 4, 5), (hg, 4, 6))
+    for buf, k, _ in halos[:6]:
         clear_outside(buf, k)
 
     barrier = pltpu.get_barrier_semaphore()
@@ -134,17 +134,15 @@
         def _():
             greet(at(a, ha, b))
 
-    @pl.loop(0, 16)
-    def _(step):
-        @pl.when(jnp.logical_not(first & (step == 0)))
-        def _():
-            greet(owner(held, lax.rem(col + step, 16)))
-
-        x, y = lax.div(step, 4), lax.rem(step, 4)
-
-        @pl.when(jnp.logical_not(first & (x == ta) & (y == low)))
-        def _():
-            greet(at(x, ha, spot * 4 + y))
+    planes = [z * 4, lax.rem(z + 1, 8) * 4]
+    for a in range(4):
+        for b in range(4):
+            itself = first & (a == ta) & (b == low)
+
+            @pl.when(jnp.logical_not(itself))
+            def _():
+                greet(at(a, ha, planes[b // 2] + b))
+                greet(at(a, ha, spot * 4 + b))
 
     near_count = 0
     for dr, dc in SIDES:
@@ -210,6 +208,9 @@
 
     def side_copy(buf, k, slot, d):
         dr, dc = SIDES[d]
+        cut = slice(None)
+        if slot > 4:
+            cut = pl.ds((slot - 5) * 2, 2)
 
         def source(side, size):
             return pl.ds(*{-1: (k, k), 0: (k, size), 1: (size, k)}[side])
@@ -218,8 +219,8 @@
             return pl.ds(*{-1: (size + k, k), 0: (k, size), 1: (0, k)}[side])
 
         return pltpu.make_async_remote_copy(
-            src_ref=buf.at[source(dr, TH), source(dc, TW)],
-            dst_ref=buf.at[target(dr, TH), target(dc, TW)],
+            src_ref=buf.at[source(dr, TH), source(dc, TW)].at[cut],
+            dst_ref=buf.at[target(dr, TH), target(dc, TW)].at[cut],
             send_sem=hsend.at[slot, d],
             recv_sem=hrecv.at[slot, d],
             device_id=near(dr, dc),
@@ -268,17 +269,20 @@
         sign = -1 if flip else 1
         return acc[2] + shifted(acc[1], sign, frames) + shifted(acc[0], 2 * sign, frames)
 
-    def conv(b):
+    def gather_taps():
         for j in range(3):
             for l in range(3):
                 at_lane = (j * 3 + l) * WIDE
                 lhs[:, at_lane : at_lane + WIDE] = (
                     af[j : j + TH, l : l + TW].reshape(512, WIDE).astype(BF16)
                 )
+
+    def conv(b, begin, rows):
         for i in range(3):
-            weights[b * 3 + i].wait()
-            pp[i] = jnp.dot(
-                lhs[...], wb[b, i].reshape(9 * WIDE, CT), preferred_element_type=F32
+            pp[i, begin : begin + rows] = jnp.dot(
+                lhs[begin : begin + rows],
+                wb[b, i].reshape(9 * WIDE, CT),
+                preferred_element_type=F32,
             )
 
     def conv_row(m):
@@ -372,7 +376,10 @@
     receive(hact, 1, 0)
     for rows, cols in ring(1):
         af[rows, cols, :, 0:CT] = hact[rows, cols].astype(F32)
-    conv(0)
+    gather_taps()
+    for copy in weights[:3]:
+        copy.wait()
+    conv(0, 0, 512)
 
     @pl.loop(0, 8)
     def _(m):
@@ -419,22 +426,29 @@
     receive(hsec, 1, 2)
     for rows, cols in ring(1):
         af[rows, cols, :, 0:CT] = hsec[rows, cols].astype(F32)
-    conv(1)
-
-    @pl.loop(0, 8)
-    def _(m):
-        h, w = lax.div(m, 2), lax.rem(m, 2) * 8
-        target = (xt[h, pl.ds(w, 8)] + conv_row(m)).reshape(64, CT)
-        span = pl.ds(m * 64, 64)
-        mb[span] = (pr[span] - target).astype(BF16)
-
-    g = jnp.dot(mb[...], projv[...], preferred_element_type=F32).reshape(4, 16, 8, CS)
-    gf[4:8, 4:20] = g
-    hg[4:8, 4:20] = g.astype(BF16)
-    send(hg, 4, 5)
+    gather_taps()
+    for copy in weights[3:]:
+        copy.wait()
+    for half in range(2):
+        conv(1, half * 256, 256)
+
+        @pl.loop(half * 4, half * 4 + 4)
+        def _(m):
+            h, w = lax.div(m, 2), lax.rem(m, 2) * 8
+            target = (xt[h, pl.ds(w, 8)] + conv_row(m)).reshape(64, CT)
+            span = pl.ds(m * 64, 64)
+            mb[span] = (pr[span] - target).astype(BF16)
+
+        g = jnp.dot(
+            mb[half * 256 : half * 256 + 256], projv[...], preferred_element_type=F32
+        ).reshape(2, 16, 8, CS)
+        gf[half * 2 + 4 : half * 2 + 6, 4:20] = g
+        hg[half * 2 + 4 : half * 2 + 6, 4:20] = g.astype(BF16)
+        send(hg, 4, 5 + half)
 
     receive(hs, 3, 4)
     receive(hg, 4, 5)
+    receive(hg, 4, 6)
     for rows, cols in ring(4):
         gf[rows, cols] = hg[rows, cols].astype(F32)
 
@@ -595,8 +609,8 @@
         dma(()),
         dma(()),
         dma(()),
-        dma((6, 8)),
-        dma((6, 8)),
+        dma((7, 8)),
+        dma((7, 8)),
     ]
     result = pl.pallas_call(
         kernel,

time: 71 us -> 66.7 us (0.939)
  Pallas kernels: 69.3 us -> 65 us
    pallas_call x1, Pallas kernels: 69.3 us -> 65 us  [on_device(): pl.pallas_call(kernel, out_shape=jax.ShapeDtypeStruct((2, 32, 8, CS), BF1...]
where the time goes in v6:
time: 66.7 us; the launch traced here: 66.5 us
  Pallas kernels  65 us (97%)
  local copies, waits for them, and re-layouts  1.57 us (2%)
    pallas_call x1, Pallas kernels, on_device(): pl.pallas_call(kernel, out_shape=jax.ShapeDtypeStruct((2, 32, 8, CS), BF1...  65 us
    unnamed x1, local copies, waits for them, and re-layouts  1.57 us

profile of v6, /device:TPU:57, one launch (start us, length us, event | category | flops | bytes accessed | tf_op | source)
XLA Modules:
  0.0 66.5 jit_solution(9688190499698546617)
XLA Ops:
  0.0 65.0 %shard_map.64 = bf16[2,32,8,128]{3,2,1,0:T(8,128)(2,1)} custom-call(bf16[2,32,8,192]{3,2,1,0:T(8,128)(2,1)} %tin.1, bf16[1,2,3,3,3,192,192]{6,5,4,3,2,1,0:T(8,128)(2,1)} %tw.1, bf16[2,32,8,128]{3,2,1,0:T(8,128)(2,1)} %bitcast.7, f32[3,3,3,4,128]{4,3,2,1,0:T(4,128)} %bitcast.8, bf16[4,128,128]{2,1,0:T(8,128)(2,1)} %pw.1, bf16[192,128]{1,0:T(8,128)(2,1)} %bitcast.9), custom_call_target="tpu_custom_call" | custom-call | tf_op jit(solution)/shard_map/pallas_call | solution.py:615
  65.0 1.6 %copy.9 = bf16[2,1,256,128]{3,2,1,0:T(8,128)(2,1)} copy(bf16[2,1,256,128]{3,2,1,0:T(8,128)(2,1)} %bitcast.6) | data formatting | bytes 262144
